TPU v7x, 128 devices: a whole 4x4x4 slice. The times are simulated.
128 devices in a mesh: lon: 32 (over y, x_hi, z), lat: 4 (over x_lo, core).
Axes of the slice: x: 4 (x_hi: 2, x_lo: 2; x = x_hi * 2 + x_lo), y: 4, z: 4, core: 2. Of those that a mesh axis runs over, the one named last changes fastest.
Arguments:
- field: bfloat16 [8, 96, 147456], P(None, 'lat', 'lon'), may hold values from -6 to 6
- cotangent: bfloat16 [8, 96, 147456], P(None, 'lat', 'lon'), may hold values from -6 to 6
- fine_gain_a: float32 [192], replicated, may hold values from 0.25 to 1.75
- fine_qkv: bfloat16 [192, 576], replicated, may hold values from -0.4375 to 0.4375
- fine_out: bfloat16 [192, 192], replicated, may hold values from -0.4375 to 0.4375
- fine_bias: bfloat16 [6, 16, 20736], P(None, 'lat'), may hold values from -6 to 6
- fine_gain_b: float32 [192], replicated, may hold values from 0.25 to 1.75
- fine_in: bfloat16 [192, 768], replicated, may hold values from -0.4375 to 0.4375
- fine_back: bfloat16 [192, 768], replicated, may hold values from -0.21875 to 0.21875
- merge_gain: float32 [768], replicated, may hold values from 0.25 to 1.75
- merge_weight: bfloat16 [768, 384], replicated, may hold values from -0.21875 to 0.21875
- coarse_gain_a: float32 [384], replicated, may hold values from 0.25 to 1.75
- coarse_qkv: bfloat16 [384, 1152], replicated, may hold values from -0.3125 to 0.3125
- coarse_out: bfloat16 [384, 384], replicated, may hold values from -0.3125 to 0.3125
- coarse_bias: bfloat16 [12, 8, 20736], P(None, 'lat'), may hold values from -6 to 6
- coarse_gain_b: float32 [384], replicated, may hold values from 0.25 to 1.75
- coarse_in: bfloat16 [384, 1536], replicated, may hold values from -0.3125 to 0.3125
- coarse_back: bfloat16 [384, 1536], replicated, may hold values from -0.15625 to 0.15625
- up_weight: bfloat16 [384, 768], replicated, may hold values from -0.3125 to 0.3125
Outputs:
- output: bfloat16 [8, 96, 147456], P(None, 'lat', 'lon')
- up_grad: float32 [384, 768], replicated
All inputs are finite; a program needn't handle non-finite values.
Results may differ from a plain program's by a relative error of at most 0.02.
Values may be sent and summed in bfloat16 or wider, within the bound.
No kernel may reach another device: no remote copies, remote signals or barrier semaphores. Data moves between devices by JAX's collectives and lax.ppermute only.
A program may use at most 128 MiB of HBM per device.

v0:
```python
import jax
import jax.numpy as jnp
from jax import lax
from jax.sharding import PartitionSpec as P


def passed_along(block, axis, distance):
    devices = range(lax.axis_size(axis))
    route = [((i - distance) % len(devices), i) for i in devices]
    return lax.ppermute(block, axis, route)


def layer_norm(value, gain):
    center = value - jnp.mean(value, axis=-1, keepdims=True)
    spread = jnp.mean(center * center, axis=-1, keepdims=True)
    return center * lax.rsqrt(spread + 1e-05) * gain


def window_block(field_in, gain_a, w_qkv, w_out, bias, gain_b, w_in, w_back):
    heads = bias.shape[0]
    levels, rows, cols, width = field_in.shape
    hdim = width // heads
    windows = field_in.reshape(levels // 2, 2, rows // 6, 6, cols // 12, 12, width)
    windows = windows.transpose(2, 0, 4, 1, 3, 5, 6).reshape(
        rows // 6, levels // 2 * (cols // 12), 144, width
    )
    tables = bias.reshape(heads, rows // 6, 144, 144).transpose(1, 0, 2, 3)

    def single(item):
        tokens, table = item
        count = tokens.shape[0]
        flat = tokens.reshape(count * 144, width).astype(jnp.float32)
        normed = layer_norm(flat, gain_a).astype(jnp.bfloat16)
        packed = jnp.dot(normed, w_qkv, preferred_element_type=jnp.float32).astype(jnp.bfloat16)
        packed = packed.reshape(count, 144, 3, heads, hdim)
        scores = jnp.einsum(
            "nqhd,nkhd->nhqk", packed[:, :, 0], packed[:, :, 1], preferred_element_type=jnp.float32
        ) * hdim ** (-0.5)
        scores = scores + table.astype(jnp.float32)[None]
        weights = jax.nn.softmax(scores, axis=-1).astype(jnp.bfloat16)
        mixed = jnp.einsum(
            "nhqk,nkhd->nqhd", weights, packed[:, :, 2], preferred_element_type=jnp.float32
        ).astype(jnp.bfloat16)
        mixed = mixed.reshape(count * 144, width)
        resid = flat + jnp.dot(mixed, w_out, preferred_element_type=jnp.float32)
        inner = layer_norm(resid, gain_b).astype(jnp.bfloat16)
        hidden = jax.nn.gelu(jnp.dot(inner, w_in, preferred_element_type=jnp.float32)).astype(
            jnp.bfloat16
        )
        result = resid + lax.dot_general(
            hidden, w_back, (((1,), (1,)), ((), ())), preferred_element_type=jnp.float32
        )
        return result.astype(jnp.bfloat16).reshape(count, 144, width)

    done = lax.map(single, (windows, tables))
    done = done.reshape(rows // 6, levels // 2, cols // 12, 2, 6, 12, width)
    return done.transpose(1, 3, 0, 4, 2, 5, 6).reshape(levels, rows, cols, width)


def group_patches(value):
    levels, rows, cols, width = value.shape
    grouped = value.reshape(levels, rows // 2, 2, cols // 2, 2, width).transpose(0, 1, 3, 2, 4, 5)
    return grouped.reshape(levels, rows // 2, cols // 2, 4 * width)


def roll_west(value, offset):
    incoming = passed_along(value[:, :, :offset], "lon", -1)
    return jnp.concatenate([value[:, :, offset:], incoming], axis=2)


def roll_east(value, offset):
    incoming = passed_along(value[:, :, -offset:], "lon", 1)
    return jnp.concatenate([incoming, value[:, :, :-offset]], axis=2)


def merge_patches(value, gain, weight):
    normed = layer_norm(group_patches(value).astype(jnp.float32), gain).astype(jnp.bfloat16)
    return jnp.dot(normed, weight, preferred_element_type=jnp.float32).astype(jnp.bfloat16)


def shards(
    field,
    cotangent,
    fine_gain_a,
    fine_qkv,
    fine_out,
    fine_bias,
    fine_gain_b,
    fine_in,
    fine_back,
    merge_gain,
    merge_weight,
    coarse_gain_a,
    coarse_qkv,
    coarse_out,
    coarse_bias,
    coarse_gain_b,
    coarse_in,
    coarse_back,
    up_weight,
):
    width = fine_qkv.shape[0]
    levels, rows = (field.shape[0], field.shape[1])
    cols = field.shape[2] // width
    field = field.reshape(levels, rows, cols, width)
    cotangent = cotangent.reshape(levels, rows, cols, width)
    fine_done = window_block(
        roll_west(field, 6),
        fine_gain_a,
        fine_qkv,
        fine_out,
        fine_bias,
        fine_gain_b,
        fine_in,
        fine_back,
    )
    settled = roll_east(fine_done, 6)
    coarse = merge_patches(settled, merge_gain, merge_weight)
    coarse_rolled = roll_west(coarse, 6)
    coarse_mid = window_block(
        coarse_rolled,
        coarse_gain_a,
        coarse_qkv,
        coarse_out,
        coarse_bias,
        coarse_gain_b,
        coarse_in,
        coarse_back,
    )
    coarse_done = roll_east(coarse_mid, 6)
    raised = jnp.dot(coarse_done, up_weight, preferred_element_type=jnp.float32)
    raised = raised.reshape(levels, rows // 2, cols // 2, 2, 2, width).transpose(0, 1, 3, 2, 4, 5)
    raised = raised.reshape(levels, rows, cols, width)
    output = (settled.astype(jnp.float32) + raised).astype(jnp.bfloat16)
    output = output.reshape(levels, rows, cols * width)
    flat_coarse = coarse_done.reshape(-1, 2 * width)
    flat_cot = group_patches(cotangent).reshape(-1, 4 * width)
    local_grad = lax.dot_general(
        flat_coarse, flat_cot, (((0,), (0,)), ((), ())), preferred_element_type=jnp.float32
    )
    up_grad = lax.psum(local_grad, ("lon", "lat"))
    return (output, up_grad)


def solution(mesh):
    return jax.shard_map(
        shards,
        mesh=mesh,
        in_specs=(
            P(None, "lat", "lon"),
            P(None, "lat", "lon"),
            P(),
            P(),
            P(),
            P(None, "lat", None),
            P(),
            P(),
            P(),
            P(),
            P(),
            P(),
            P(),
            P(),
            P(None, "lat", None),
            P(),
            P(),
            P(),
            P(),
        ),
        out_specs=(P(None, "lat", "lon"), P()),
        check_vma=False,
    )
```

profile of v0, /device:TPU:1, one launch (start us, length us, event | category | flops | bytes accessed | tf_op | source)
XLA Modules:
  0.0 534.4 jit_solution(14968533061270977272)
XLA Ops:
  7.2 3.5 reshape.196
  12.0 9.5 %collective-permute-start = (bf16[8,24,6,192]{3,0,2,1:T(8,128)(2,1)}, bf16[8,24,6,192]{3,0,2,1:T(8,128)(2,1)S(1)}, u32[]{:S(2)}, u32[]{:S(2)}) collective-permute-start(bf16[8,24,6,192]{3,0,2,1:T(8,128)(2,1)} %copy.147), channel_id=1, source_target_pairs={{4,0},{8,4},{12,8},{16,12},{20,16},{24,20},{28,24},{32,28},{36,32}... | collective-permute-start | bytes 1327112 | tf_op jit(solution)/shard_map/ppermute | solution.py:10
  24.2 3.9 copy.146
  28.1 4.2 reshape.199
  38.2 3.5 copy.109
  43.5 130.9 %while.20 = (s32[]{:T(128)}, bf16[4,8,144,192]{3,2,1,0:T(8,128)(2,1)}, bf16[4,8,144,192]{3,2,1,0:T(8,128)(2,1)}, f32[192]{0:T(256)S(1)}, bf16[192,576]{1,0:T(8,1...) while((s32[]{:T(128)}, ...), condition=%wide.region_7.8_spmd, body=%wide.region_0.7_spmd.sunk | while | flops 1166430080 | bytes 37934784 | solution.py:55
  53.7 4.5 reshape.224
  59.7 7.4 %fusion.125 = (f32[8,6,144]{2,1,0:T(8,128)S(1)}, f32[8,6,144,144]{2,3,1,0:T(8,128)}) fusion(f32[6,144,144]{1,2,0:T(8,128)} %bitcast_convert_fusion.4, bf16[8,144,1,6,32]{1,0,4,3,2:T(8,128)(2,1)} %get-tuple-element.352, bf16[8,144,1,6,32]{1,0,4,3,2:T(8,128)(2,1)} %get-tuple-element.353), kind=kOutput, calls=%fused_computation.125.clone.1 | convolution fusion | flops 67682448 | bytes 5391360 | tf_op jit(solution)/shard_map/while/body/eval_jaxpr/sub | solution.py:40
  67.1 3.7 fusion.126
  72.5 2.7 fusion.128
  86.3 4.5 reshape.224
  92.3 7.4 %fusion.125 = (f32[8,6,144]{2,1,0:T(8,128)S(1)}, f32[8,6,144,144]{2,3,1,0:T(8,128)}) fusion(f32[6,144,144]{1,2,0:T(8,128)} %bitcast_convert_fusion.4, bf16[8,144,1,6,32]{1,0,4,3,2:T(8,128)(2,1)} %get-tuple-element.352, bf16[8,144,1,6,32]{1,0,4,3,2:T(8,128)(2,1)} %get-tuple-element.353), kind=kOutput, calls=%fused_computation.125.clone.1 | convolution fusion | flops 67682448 | bytes 5391360 | tf_op jit(solution)/shard_map/while/body/eval_jaxpr/sub | solution.py:40
  99.7 3.7 fusion.126
  118.8 4.5 reshape.224
  124.8 7.4 %fusion.125 = (f32[8,6,144]{2,1,0:T(8,128)S(1)}, f32[8,6,144,144]{2,3,1,0:T(8,128)}) fusion(f32[6,144,144]{1,2,0:T(8,128)} %bitcast_convert_fusion.4, bf16[8,144,1,6,32]{1,0,4,3,2:T(8,128)(2,1)} %get-tuple-element.352, bf16[8,144,1,6,32]{1,0,4,3,2:T(8,128)(2,1)} %get-tuple-element.353), kind=kOutput, calls=%fused_computation.125.clone.1 | convolution fusion | flops 67682448 | bytes 5391360 | tf_op jit(solution)/shard_map/while/body/eval_jaxpr/sub | solution.py:40
  132.2 3.7 fusion.126
  151.3 4.5 reshape.224
  157.3 7.4 %fusion.125 = (f32[8,6,144]{2,1,0:T(8,128)S(1)}, f32[8,6,144,144]{2,3,1,0:T(8,128)}) fusion(f32[6,144,144]{1,2,0:T(8,128)} %bitcast_convert_fusion.4, bf16[8,144,1,6,32]{1,0,4,3,2:T(8,128)(2,1)} %get-tuple-element.352, bf16[8,144,1,6,32]{1,0,4,3,2:T(8,128)(2,1)} %get-tuple-element.353), kind=kOutput, calls=%fused_computation.125.clone.1 | convolution fusion | flops 67682448 | bytes 5391360 | tf_op jit(solution)/shard_map/while/body/eval_jaxpr/sub | solution.py:40
  164.7 3.7 fusion.126
  174.4 3.5 copy.112
  177.9 3.8 copy.113
  181.8 5.0 reshape.201
  187.1 19.8 %collective-permute-done.1 = bf16[8,24,6,192]{3,0,2,1:T(8,128)(2,1)S(1)} collective-permute-done((bf16[8,24,6,192]{3,0,2,1:T(8,128)(2,1)S(1)}, bf16[8,24,6,192]{3,0,2,1:T(8,128)(2,1)S(1)}, u32[]{:S(2)}, u32[]{:S(2)}) %collective-permute-start.1) | collective-permute-done | bytes 442400 | tf_op jit(solution)/shard_map/ppermute | solution.py:10
  207.4 4.8 copy.210
  212.1 3.3 fusion.76
  215.5 7.2 %reshape.215 = f32[8,12,12,768]{3,0,2,1:T(8,128)} reshape(f32[8,12,12,2,2,192]{5,4,3,0,2,1:T(2,128)} %bitcast.194) | data formatting | bytes 7077888 | tf_op jit(solution)/shard_map/convert_element_type | solution.py:77
  222.7 10.7 %multiply_reduce_fusion.4 = f32[8,12,12]{0,2,1:T(8,128)S(1)} fusion(f32[8,12,12]{0,2,1:T(8,128)S(1)} %broadcast_multiply_fusion.4, f32[8,12,2,12,2,192]{5,0,4,3,2,1:T(8,128)} %bitcast.191), kind=kLoop, calls=%fused_computation.106 | loop fusion | flops 2653056 | bytes 3548160 | tf_op jit(solution)/shard_map/reduce_sum | solution.py:15
  237.6 4.3 reshape.204
  241.9 4.0 collective-permute-done.2
  248.1 72.6 %while.21 = (s32[]{:T(128)}, bf16[2,4,144,384]{3,1,2,0:T(4,128)(2,1)}, bf16[2,4,144,384]{3,1,2,0:T(4,128)(2,1)}, f32[384]{0:T(512)S(1)}, bf16[384,1152]{1,0:T(8,...) while((s32[]{:T(128)}, ...), condition=%wide.region_17.18_spmd, body=%wide.region_10.17_spmd.sunk | while | flops 2185769216 | bytes 58114856 | solution.py:55
  258.6 5.1 reshape.226
  266.0 7.7 %fusion.136 = (f32[4,12,144]{2,1,0:T(8,128)S(1)}, f32[4,12,144,144]{2,3,1,0:T(8,128)}) fusion(f32[12,144,144]{1,2,0:T(8,128)} %bitcast_convert_fusion.5, bf16[4,144,1,12,32]{1,0,4,3,2:T(4,128)(2,1)} %get-tuple-element.369, bf16[4,144,1,12,32]{1,0,4,3,2:T(4,128)(2,1)} %get-tuple-element.370), kind=kOutput, calls=%fused_computation.128.clone.1 | convolution fusion | flops 67682448 | bytes 5889024 | tf_op jit(solution)/shard_map/while/body/eval_jaxpr/sub | solution.py:40
  273.6 3.6 fusion.137
  279.3 3.8 fusion.139
  294.6 5.1 reshape.226
  302.0 7.7 %fusion.136 = (f32[4,12,144]{2,1,0:T(8,128)S(1)}, f32[4,12,144,144]{2,3,1,0:T(8,128)}) fusion(f32[12,144,144]{1,2,0:T(8,128)} %bitcast_convert_fusion.5, bf16[4,144,1,12,32]{1,0,4,3,2:T(4,128)(2,1)} %get-tuple-element.369, bf16[4,144,1,12,32]{1,0,4,3,2:T(4,128)(2,1)} %get-tuple-element.370), kind=kOutput, calls=%fused_computation.128.clone.1 | convolution fusion | flops 67682448 | bytes 5889024 | tf_op jit(solution)/shard_map/while/body/eval_jaxpr/sub | solution.py:40
  309.6 3.6 fusion.137
  315.3 3.8 fusion.139
  323.4 3.1 reshape_reshape.6
  326.5 3.4 copy.211
  332.7 6.0 %copy.114 = f32[8,24,24,192]{3,2,1,0:T(8,128)} copy(f32[8,24,24,192]{3,0,2,1:T(8,128)} %copy-done.3) | data formatting | bytes 7077888 | tf_op jit(solution)/shard_map/convert_element_type | solution.py:134
  338.7 5.5 %reshape.214 = f32[8,24,4608]{2,1,0:T(8,128)} reshape(f32[8,24,24,192]{3,2,1,0:T(8,128)} %copy.114) | data formatting | bytes 7077888 | tf_op jit(solution)/shard_map/convert_element_type | solution.py:134
  345.9 3.1 fusion.72
  349.0 7.6 %reshape.207 = f32[8,12,12,2,2,192]{5,4,3,0,2,1:T(2,128)} reshape(f32[8,12,12,768]{3,0,2,1:T(8,128)} %fusion.72) | data formatting | bytes 7077888 | tf_op jit(solution)/shard_map/reshape | solution.py:132
  356.6 7.2 %copy.127 = f32[8,12,2,12,2,192]{5,4,3,2,1,0:T(2,128)} copy(f32[8,12,2,12,2,192]{5,4,2,0,3,1:T(2,128)} %bitcast.195) | data formatting | bytes 7077888 | tf_op jit(solution)/shard_map/transpose | solution.py:132
  363.9 7.0 %reshape.208 = f32[8,24,4608]{2,1,0:T(8,128)} reshape(f32[8,12,2,12,2,192]{5,4,3,2,1,0:T(2,128)} %copy.127) | data formatting | bytes 7077888 | tf_op jit(solution)/shard_map/reshape | solution.py:133
  372.9 4.6 add_convert_fusion
  377.5 147.4 %all-reduce.2.cloned.1.call-done = f32[384,768]{1,0:T(8,128)} async-done(((f32[384,768]{1,0:T(8,128)}), f32[384,768]{1,0:T(8,128)}) %all-reduce.2.cloned.1.call-update) | async-done | bytes 1179664 | tf_op jit(solution)/shard_map/psum | solution.py:141
  (237 shorter events, 125.9 us)
Async XLA Ops:
  7.2 338.8 %copy-start = (bf16[384,768]{1,0:T(8,128)(2,1)S(1)}, bf16[384,768]{1,0:T(8,128)(2,1)}, u32[]{:S(2)}) copy-start(bf16[384,768]{1,0:T(8,128)(2,1)} %param.41) | copy-start | bytes 1769476
  7.2 517.8 %all-reduce.2.cloned.1.call-start = ((), (), s32[]{:S(2)}) async-start(), calls=%async_computation | async-start | bytes 2359296 | tf_op jit(solution)/shard_map/psum | solution.py:141
  12.0 21.8 %collective-permute-start = (bf16[8,24,6,192]{3,0,2,1:T(8,128)(2,1)}, bf16[8,24,6,192]{3,0,2,1:T(8,128)(2,1)S(1)}, u32[]{:S(2)}, u32[]{:S(2)}) collective-permute-start(bf16[8,24,6,192]{3,0,2,1:T(8,128)(2,1)} %copy.147), channel_id=1, source_target_pairs={{4,0},{8,4},{12,8},{16,12},{20,16},{24,20},{28,24},{32,28},{36,32}... | collective-permute-start | bytes 1327112 | tf_op jit(solution)/shard_map/ppermute | solution.py:10
  24.2 4.0 copy-start.14
  41.7 1.8 copy-start.11
  41.7 1.8 copy-start.12
  41.7 1.8 copy-start.19
  41.7 1.8 copy-start.23
  59.7 7.4 %copy-start.6 = (bf16[8,144,1,6,32]{1,0,4,3,2:T(8,128)(2,1)S(1)}, bf16[8,144,1,6,32]{1,0,4,3,2:T(8,128)(2,1)}, u32[]{:S(2)}) copy-start(bf16[8,144,1,6,32]{1,0,4,3,2:T(8,128)(2,1)} %get-tuple-element.356) | copy-start | bytes 1327108 | tf_op jit(solution)/shard_map/while
  70.8 1.2 copy-start.4
  92.3 7.4 %copy-start.6 = (bf16[8,144,1,6,32]{1,0,4,3,2:T(8,128)(2,1)S(1)}, bf16[8,144,1,6,32]{1,0,4,3,2:T(8,128)(2,1)}, u32[]{:S(2)}) copy-start(bf16[8,144,1,6,32]{1,0,4,3,2:T(8,128)(2,1)} %get-tuple-element.356) | copy-start | bytes 1327108 | tf_op jit(solution)/shard_map/while
  103.4 1.2 copy-start.4
  124.8 7.4 %copy-start.6 = (bf16[8,144,1,6,32]{1,0,4,3,2:T(8,128)(2,1)S(1)}, bf16[8,144,1,6,32]{1,0,4,3,2:T(8,128)(2,1)}, u32[]{:S(2)}) copy-start(bf16[8,144,1,6,32]{1,0,4,3,2:T(8,128)(2,1)} %get-tuple-element.356) | copy-start | bytes 1327108 | tf_op jit(solution)/shard_map/while
  135.9 1.2 copy-start.4
  157.3 7.4 %copy-start.6 = (bf16[8,144,1,6,32]{1,0,4,3,2:T(8,128)(2,1)S(1)}, bf16[8,144,1,6,32]{1,0,4,3,2:T(8,128)(2,1)}, u32[]{:S(2)}) copy-start(bf16[8,144,1,6,32]{1,0,4,3,2:T(8,128)(2,1)} %get-tuple-element.356) | copy-start | bytes 1327108 | tf_op jit(solution)/shard_map/while
  168.4 1.2 copy-start.4
  186.9 20.0 %collective-permute-start.1 = (bf16[8,24,6,192]{3,0,2,1:T(8,128)(2,1)S(1)}, bf16[8,24,6,192]{3,0,2,1:T(8,128)(2,1)S(1)}, u32[]{:S(2)}, u32[]{:S(2)}) collective-permute-start(bf16[8,24,6,192]{3,0,2,1:T(8,128)(2,1)S(1)} %slice.58), channel_id=1, source_target_pairs={{124,0},{0,4},{4,8},{8,12},{12,16},{16,20},{20,24},{24,28},{28,32}... | collective-permute-start | bytes 1327112 | tf_op jit(solution)/shard_map/ppermute | solution.py:10
  207.4 4.8 copy-start.3
  222.7 10.8 %copy-start.8 = (f32[8,12,12,768]{3,0,2,1:T(8,128)S(1)}, f32[8,12,12,768]{3,0,2,1:T(8,128)}, u32[]{:S(2)}) copy-start(f32[8,12,12,768]{3,0,2,1:T(8,128)} %reshape.215) | copy-start | bytes 10616836
  222.7 10.8 %copy-start.20 = (f32[768]{0:T(1024)S(1)}, f32[768]{0:T(1024)}, u32[]{:S(2)}) copy-start(f32[768]{0:T(1024)} %param.32) | copy-start | bytes 9220
  233.5 1.1 copy-start.21
  235.9 1.7 copy-start.15
  236.4 9.5 %collective-permute-start.2 = (bf16[8,12,6,384]{3,0,2,1:T(8,128)(2,1)S(1)}, bf16[8,12,6,384]{3,0,2,1:T(8,128)(2,1)S(1)}, u32[]{:S(2)}, u32[]{:S(2)}) collective-permute-start(bf16[8,12,6,384]{3,0,2,1:T(8,128)(2,1)S(1)} %copy.117), channel_id=1, source_target_pairs={{4,0},{8,4},{12,8},{16,12},{20,16},{24,20},{28,24},{32,28},{36,32}... | collective-permute-start | bytes 1327112 | tf_op jit(solution)/shard_map/ppermute | solution.py:10
  246.0 2.1 copy-start.9
  246.0 2.1 copy-start.18
  246.0 2.1 copy-start.22
  248.3 1.6 copy-start.5
  249.7 5.2 copy-start.1
  266.0 7.7 %copy-start.7 = (bf16[4,144,1,12,32]{1,0,4,3,2:T(4,128)(2,1)S(1)}, bf16[4,144,1,12,32]{1,0,4,3,2:T(4,128)(2,1)}, u32[]{:S(2)}) copy-start(bf16[4,144,1,12,32]{1,0,4,3,2:T(4,128)(2,1)} %get-tuple-element.373) | copy-start | bytes 1327108 | tf_op jit(solution)/shard_map/while
  277.3 1.2 copy-start.2
  279.3 3.9 copy-start.16
  283.4 0.9 copy-start.17
  284.3 1.6 copy-start.5
  285.7 5.2 copy-start.1
  302.0 7.7 %copy-start.7 = (bf16[4,144,1,12,32]{1,0,4,3,2:T(4,128)(2,1)S(1)}, bf16[4,144,1,12,32]{1,0,4,3,2:T(4,128)(2,1)}, u32[]{:S(2)}) copy-start(bf16[4,144,1,12,32]{1,0,4,3,2:T(4,128)(2,1)} %get-tuple-element.373) | copy-start | bytes 1327108 | tf_op jit(solution)/shard_map/while
  313.3 1.2 copy-start.2
  315.3 3.9 copy-start.16
  319.4 0.9 copy-start.17
  320.7 2.7 copy-start.13
  323.3 20.8 %collective-permute-start.3 = (bf16[8,12,6,384]{3,0,2,1:T(8,128)(2,1)}, bf16[8,12,6,384]{3,0,2,1:T(8,128)(2,1)}, u32[]{:S(2)}, u32[]{:S(2)}) collective-permute-start(bf16[8,12,6,384]{3,0,2,1:T(8,128)(2,1)} %copy.124), channel_id=1, source_target_pairs={{124,0},{0,4},{4,8},{8,12},{12,16},{16,20},{20,24},{24,28},{28,32}... | collective-permute-start | bytes 1327112 | tf_op jit(solution)/shard_map/ppermute | solution.py:10
  363.9 7.0 %copy-start.10 = (bf16[1152,768]{1,0:T(8,128)(2,1)S(1)}, bf16[1152,768]{1,0:T(8,128)(2,1)}, u32[]{:S(2)}) copy-start(bf16[1152,768]{1,0:T(8,128)(2,1)} %reshape_reshape.7) | copy-start | bytes 5308420
Sparse Core Ops, SparseCore 0:
  373.0 151.9 all-reduce.1
where the time goes:
time: 543 us; the launch traced here: 534 us
  local copies, waits for them, and re-layouts  177 us (33%)
  waiting for transfers between devices  173 us (32%)
  matrix products  106 us (20%)
  other arithmetic  51 us (9%)
  between operations  14.5 us (3%)
  starting transfers between devices  10.9 us (2%)
    psum x1, waiting for transfers between devices, shards(): up_grad = lax.psum(local_grad, ('lon', 'lat'))  147 us
    sub x6, matrix products, single(): weights = jax.nn.softmax(scores, axis=-1).astype(jnp.bfloat16)  45 us
    reshape x6, local copies, waits for them, and re-layouts, single(): packed = packed.reshape(count, 144, 3, heads, hdim)  28.2 us
    ppermute x4, waiting for transfers between devices, passed_along(): return lax.ppermute(block, axis, route)  25.2 us
    dot_general x6, matrix products, single(): jnp.einsum('nhqk,nkhd->nqhd', weights, packed[:, :, 2], preferred_element...  22 us
    reduce_sum x13, other arithmetic, layer_norm(): spread = jnp.mean(center * center, axis=-1, keepdims=True)  19 us
    dot_general x6, matrix products, single(): lax.dot_general(hidden, w_back, (((1,), (1,)), ((), ())), preferred_eleme...  18.6 us
    convert_element_type x2, local copies, waits for them, and re-layouts, merge_patches(): group_patches(value).astype(jnp.float32)  12 us
  transfers between devices with their start and end apart: 5, of which 4 were waited for; matrix products, arithmetic and copies ran while one was open for 8% of the time, Pallas kernels for 0%

commit v1 on v0

v1 whole, which is shorter than its diff:
```python
import functools
import jax
import jax.numpy as jnp
from jax import lax
from jax.experimental import pallas as pl
from jax.experimental.pallas import tpu as pltpu
from jax.sharding import PartitionSpec as P

BF = jnp.bfloat16
F32 = jnp.float32
NN = (((1,), (0,)), ((), ()))
NT = (((1,), (1,)), ((), ()))
TN = (((0,), (0,)), ((), ()))
LOG2E = 1.4426950408889634
HD = 32
UNITS = 2
LEAD = 0
MIB = 1024 * 1024


def mm(a, b, dims=NN):
    return lax.dot_general(a, b, dims, preferred_element_type=F32)


def row(ref):
    return ref[...].reshape(1, ref.shape[0])


def layer_norm(value, gain):
    center = value - jnp.mean(value, axis=-1, keepdims=True)
    spread = jnp.mean(center * center, axis=-1, keepdims=True)
    return center * lax.rsqrt(spread + 1e-05) * gain


def scaled_bias(bias_ref, table_ref, heads):
    for h in range(heads):
        for w in range(bias_ref.shape[1]):
            table_ref[w * heads + h] = bias_ref[h, w].astype(F32) * LOG2E


def put_rows(ref, at, value):
    for t in range(value.shape[1] // 128):
        ref[t, at : at + value.shape[0], :] = value[:, t * 128 : (t + 1) * 128]


def get_rows(ref, at, count):
    return jnp.concatenate([ref[t, at : at + count, :] for t in range(ref.shape[0])], axis=1)


def get_every_other(ref, at, count):
    return jnp.concatenate([ref[t, pl.ds(at, count, stride=2), :] for t in range(ref.shape[0])], axis=1)


def put_every_other(ref, at, value):
    for t in range(ref.shape[0]):
        ref[t, pl.ds(at, value.shape[0], stride=2), :] = value[:, t * 128 : (t + 1) * 128]


def tiled(value):
    short = -value.shape[1] % 128
    if short:
        value = jnp.concatenate([value, jnp.zeros((value.shape[0], short), value.dtype)], axis=1)
    return value


def window_block(result, v, ga, wq, wk, wv, w_out, table_ref, gb, w_in, w_back, mixed_ref):
    tokens, width = v.shape
    heads = width // HD
    aw = layer_norm(v, ga).astype(BF)
    yield
    q_all = (mm(aw, wq) * (LOG2E * HD**-0.5)).astype(BF)
    k_all = mm(aw, wk).astype(BF)
    v_all = mm(aw, wv).astype(BF)
    yield
    lane = lax.broadcasted_iota(jnp.int32, (144, 128), 1)
    ones = jnp.ones((144, 128), BF)
    for w in range(tokens // 144):
        rows = slice(w * 144, (w + 1) * 144)
        for t in range(-(-width // 128)):
            lanes = slice(t * 128, t * 128 + 128)
            total = jnp.zeros((144, 128), F32)
            count = jnp.ones((144, 128), F32)
            q, k = q_all[rows, lanes], k_all[rows, lanes]
            values = jnp.concatenate([v_all[rows, lanes], ones], axis=1)
            for j in range(min(4, heads - 4 * t)):
                mine = (lane >= j * HD) & (lane < j * HD + HD)
                s = mm(jnp.where(mine, q, jnp.zeros_like(q)), k, NT) + table_ref[w * heads + 4 * t + j]
                p = jnp.exp2(s - jnp.max(s, axis=1, keepdims=True)).astype(BF)
                o = mm(p, values)
                total = jnp.where(mine, o[:, :128], total)
                count = jnp.where(mine, o[:, 128:], count)
            mixed_ref[rows, lanes] = (total / count).astype(BF)
            yield
    r = v + mm(mixed_ref[:, :width], w_out)
    m = layer_norm(r, gb).astype(BF)
    yield
    u = jax.nn.gelu(mm(m, w_in)).astype(BF)
    yield
    result.append((r + mm(u, w_back, NT)).astype(BF))
    yield


def interleave(streams, lead):
    waiting = list(streams)
    for _ in range(lead):
        next(waiting[0], None)
    while waiting:
        waiting = [g for g in waiting if next(g, g) is not g]


def fine_moves():
    for l in range(2):
        for row in range(24):
            for c in range(2):
                yield l * 288 + c * 144 + row, (row // 6) * 144 + l * 72 + (row % 6) * 12 + c


def fine_kernel(
    left_ref, right_ref, bias_ref, ga_ref, wqkv_ref, wo_ref, gb_ref,
    wi_ref, wb_ref, mg_ref, mw_ref,
    out_left, out_right, coarse_left, coarse_right, nat_ref, win_ref, table_ref, mixed_ref, proj_ref,
):
    heads = bias_ref.shape[0]

    @pl.when(pl.program_id(0) == 0)
    def _():
        scaled_bias(bias_ref, table_ref, heads)
        width = wo_ref.shape[0]
        proj_ref[...] = jnp.zeros_like(proj_ref)
        for i in range(3):
            proj_ref[i, :, :width] = wqkv_ref[:, i * width : (i + 1) * width]

    units = left_ref.shape[0] // 2
    interleave(
        [
            fine_unit(
                u, (left_ref, right_ref), ga_ref, proj_ref, wo_ref, gb_ref, wi_ref, wb_ref, mg_ref, mw_ref,
                (out_left, out_right), coarse_left, coarse_right, nat_ref.at[u], win_ref.at[u], table_ref, mixed_ref.at[u],
            )
            for u in range(units)
        ],
        LEAD if units > 1 else 0,
    )


def fine_unit(
    u, halves, ga_ref, proj_ref, wo_ref, gb_ref, wi_ref, wb_ref, mg_ref, mw_ref,
    outs, coarse_left, coarse_right, nat_ref, win_ref, table_ref, mixed_ref,
):
    width = wo_ref.shape[0]
    pair = 2 * width
    for l in range(2):
        for s in range(2):
            for p in range(3):
                at = l * 288 + (s * 3 + p) * 24
                x = halves[s][2 * u + l, :, p * pair : (p + 1) * pair].astype(F32)
                put_rows(nat_ref, at, x[:, :256])
                put_rows(nat_ref, at + 144, pltpu.roll(x[:, 128:], 192, axis=1))
    for src, dst in fine_moves():
        for t in range(2):
            win_ref[t, pl.ds(dst, 6, stride=2), :] = nat_ref[t, pl.ds(src, 6, stride=24), :]
    v = get_rows(win_ref, 0, 576)[:, :width]
    yield
    result = []
    yield from window_block(
        result, v, row(ga_ref), proj_ref[0], proj_ref[1], proj_ref[2], wo_ref[...],
        table_ref, row(gb_ref), wi_ref[...], wb_ref[...], mixed_ref,
    )
    done = result[0].astype(F32)
    put_rows(win_ref, 0, tiled(done))
    for src, dst in fine_moves():
        for t in range(2):
            nat_ref[t, pl.ds(src, 6, stride=24), :] = win_ref[t, pl.ds(dst, 6, stride=2), :]
    yield
    quarter = []
    for r in range(2):
        for c in range(2):
            quarter.append(
                jnp.concatenate(
                    [get_every_other(nat_ref, l * 288 + c * 144 + r, 72)[:, :width] for l in range(2)], axis=0
                )
            )
    mean = sum(jnp.sum(x, axis=-1, keepdims=True) for x in quarter) * (1.0 / (4 * width))
    center = [x - mean for x in quarter]
    spread = sum(jnp.sum(x * x, axis=-1, keepdims=True) for x in center) * (1.0 / (4 * width))
    scale = lax.rsqrt(spread + 1e-05)
    gains = row(mg_ref)
    coarse = 0.0
    for i in range(4):
        n = (center[i] * scale * gains[:, i * width : (i + 1) * width]).astype(BF)
        coarse = coarse + mm(n, mw_ref[i * width : (i + 1) * width])
    for l in range(2):
        coarse_left[u, l] = coarse[l * 72 : l * 72 + 36].astype(BF)
        coarse_right[u, l] = coarse[l * 72 + 36 : l * 72 + 72].astype(BF)
    yield
    low = lax.broadcasted_iota(jnp.int32, (24, 128), 1) < 64
    for l in range(2):
        for s in range(2):
            for p in range(3):
                at = l * 288 + (s * 3 + p) * 24
                even = get_rows(nat_ref, at, 24)
                odd = pltpu.roll(get_rows(nat_ref, at + 144, 24), 64, axis=1)
                middle = jnp.where(low, even[:, 128:], odd[:, :128])
                outs[s][2 * u + l, :, p * pair : (p + 1) * pair] = jnp.concatenate(
                    [even[:, :128], middle, odd[:, 128:]], axis=1
                ).astype(BF)


def coarse_kernel(
    g0, g1, g2, g3, cot_ref, cot_next_ref, bias_ref, ga_ref, wqkv_ref, wo_ref, gb_ref,
    wi_ref, wb_ref,
    done_own, done_first, done_last, packed_ref, nat_ref, win_ref, table_ref, mixed_ref, grad_ref,
):
    heads = bias_ref.shape[0]

    @pl.when(pl.program_id(0) == 0)
    def _():
        scaled_bias(bias_ref, table_ref, heads)
        grad_ref[...] = jnp.zeros_like(grad_ref)

    units = g0.shape[0]
    interleave(
        [
            coarse_unit(
                u, (g0, g1, g2, g3), cot_ref, cot_next_ref, ga_ref, wqkv_ref, wo_ref, gb_ref, wi_ref, wb_ref,
                done_own, done_last, grad_ref, nat_ref.at[u], win_ref.at[u], table_ref, mixed_ref.at[u],
            )
            for u in range(units)
        ],
        LEAD if units > 1 else 0,
    )

    @pl.when(pl.program_id(0) == 0)
    def _():
        done_first[...] = done_last[...]

    @pl.when(pl.program_id(0) == pl.num_programs(0) - 1)
    def _():
        for j in range(128):
            t, b = divmod(j, 24)
            packed_ref[j, :16, :] = grad_ref[b * 16 : b * 16 + 16, t * 128 : (t + 1) * 128].astype(BF)
            packed_ref[j, 16:, :] = grad_ref[128 + 2 * j : 130 + 2 * j, 640:].astype(BF)


def sum_kernel(in_ref, out_ref):
    total = in_ref[0].astype(F32)
    for j in range(1, 128):
        total = total + in_ref[j].astype(F32)
    total = total.astype(BF)
    for j in range(128):
        out_ref[j] = total


def unpack_kernel(in_ref, out_ref):
    for j in range(128):
        t, b = divmod(j, 24)
        out_ref[b * 16 : b * 16 + 16, t * 128 : (t + 1) * 128] = in_ref[j, :16, :].astype(F32)
        out_ref[128 + 2 * j : 130 + 2 * j, 640:] = in_ref[j, 16:, :].astype(F32)


def coarse_unit(
    u, groups, cot_ref, cot_next_ref, ga_ref, wqkv_ref, wo_ref, gb_ref, wi_ref, wb_ref,
    done_own, done_next, grad_ref, nat_ref, win_ref, table_ref, mixed_ref,
):
    width = wo_ref.shape[0]
    for l in range(2):
        for i, g in enumerate(groups):
            put_rows(nat_ref, l * 144 + i * 36, g[u, l].astype(F32))
    moves = [(l * 144 + row, (row // 6) * 144 + l * 72 + (row % 6) * 12) for l in range(2) for row in range(12)]
    for src, dst in moves:
        for t in range(3):
            win_ref[t, dst : dst + 12, :] = nat_ref[t, pl.ds(src, 12, stride=12), :]
    yield
    result = []
    yield from window_block(
        result, get_rows(win_ref, 0, 288), row(ga_ref), wqkv_ref[:, :width], wqkv_ref[:, width : 2 * width],
        wqkv_ref[:, 2 * width :], wo_ref[...],
        table_ref, row(gb_ref), wi_ref[...], wb_ref[...], mixed_ref,
    )
    done = result[0]
    put_rows(win_ref, 0, done.astype(F32))
    for src, dst in moves:
        for t in range(3):
            nat_ref[t, pl.ds(src, 12, stride=12), :] = win_ref[t, dst : dst + 12, :]
    yield
    for half, ref, out in ((0, cot_ref, done_own), (1, cot_next_ref, done_next)):
        tokens = jnp.concatenate([get_rows(nat_ref, l * 144 + half * 72, 72) for l in range(2)], axis=0).astype(BF)
        out[u] = tokens
        for l in range(2):
            for c in range(6):
                put_rows(win_ref, (l * 6 + c) * 24, ref[2 * u + l, :, c * width : (c + 1) * width].astype(F32))
        for r in range(2):
            x = get_every_other(win_ref, r, 144).astype(BF)
            grad_ref[:, r * width : (r + 1) * width] += mm(tokens, x, TN)
        yield


def final_kernel(done_west, done_east, set0, set1, set2, set3, up_ref, *rest):
    out_ref, rows_ref = rest[-2:]
    width = done_west.shape[2]
    halves = (set0, set1, set2, set3)
    for e, done_ref in enumerate((done_west, done_east)):
        raised = mm(done_ref[0], up_ref[...])
        for r in range(2):
            put_every_other(rows_ref, r, raised[:, r * width : (r + 1) * width])
        for l in range(2):
            for c in range(6):
                base = halves[2 * e + c // 3][l, :, (c % 3) * width : (c % 3 + 1) * width]
                total = base.astype(F32) + get_rows(rows_ref, (l * 6 + c) * 24, 24)
                out_ref[l, :, (e * 6 + c) * width : (e * 6 + c + 1) * width] = total.astype(BF)


def whole(a):
    return pl.BlockSpec(a.shape, lambda i: (0,) * a.ndim)


def params(mib):
    return pltpu.CompilerParams(vmem_limit_bytes=mib * MIB, dimension_semantics=("arbitrary",))


def fine_call(left, left_at, right, right_at, consts):
    levels, rows, _ = left.shape
    half = 1152
    steps = levels // (2 * UNITS)

    def spec(at):
        return pl.BlockSpec((2 * UNITS, rows, half), lambda i: (i, 0, at))

    cspec = pl.BlockSpec((UNITS, 2, 36, 384), lambda i: (i, 0, 0, 0))
    return pl.pallas_call(
        fine_kernel,
        grid=(steps,),
        in_specs=[spec(left_at), spec(right_at)] + [whole(c) for c in consts],
        out_specs=[spec(0), spec(0), cspec, cspec],
        out_shape=[jax.ShapeDtypeStruct((levels, rows, half), BF)] * 2
        + [jax.ShapeDtypeStruct((steps * UNITS, 2, 36, 384), BF)] * 2,
        scratch_shapes=[
            pltpu.VMEM((UNITS, 2, 576, 128), F32),
            pltpu.VMEM((UNITS, 2, 576, 128), F32),
            pltpu.VMEM((24, 144, 144), F32),
            pltpu.VMEM((UNITS, 576, 256), BF),
            pltpu.VMEM((3, 192, 256), BF),
        ],
        compiler_params=params(56),
        cost_estimate=pl.CostEstimate(flops=3 * 10**9, bytes_accessed=6 * 10**6, transcendentals=10**6),
    )(left, right, *consts)


def coarse_call(groups, cot, cot_next, consts):
    steps = groups[0].shape[0] // UNITS
    gspec = pl.BlockSpec((UNITS, 2, 36, 384), lambda i: (i, 0, 0, 0))
    dspec = pl.BlockSpec((UNITS, 144, 384), lambda i: (i, 0, 0))
    return pl.pallas_call(
        coarse_kernel,
        grid=(steps,),
        in_specs=[gspec] * 4
        + [pl.BlockSpec((2 * UNITS, 24, 2304), lambda i: (i, 0, 1)), pl.BlockSpec((2 * UNITS, 24, 2304), lambda i: (i, 0, 0))]
        + [whole(c) for c in consts],
        out_specs=[dspec] + [pl.BlockSpec((UNITS, 144, 384), lambda i: (0, 0, 0))] * 2
        + [pl.BlockSpec((128, 18, 128), lambda i: (0, 0, 0))],
        out_shape=[jax.ShapeDtypeStruct((steps * UNITS, 144, 384), BF)]
        + [jax.ShapeDtypeStruct((UNITS, 144, 384), BF)] * 2
        + [jax.ShapeDtypeStruct((128, 18, 128), BF)],
        scratch_shapes=[
            pltpu.VMEM((UNITS, 3, 288, 128), F32),
            pltpu.VMEM((UNITS, 3, 288, 128), F32),
            pltpu.VMEM((24, 144, 144), F32),
            pltpu.VMEM((UNITS, 288, 384), BF),
            pltpu.VMEM((384, 768), F32),
        ],
        compiler_params=params(56),
        cost_estimate=pl.CostEstimate(flops=5 * 10**9, bytes_accessed=8 * 10**6, transcendentals=10**6),
    )(*groups, cot, cot_next, *consts)


def final_call(first, done_west, done_east, quarters, up, below=None):
    steps = done_west.shape[0]
    sspec = pl.BlockSpec((2, 24, 1152), lambda i: (i + first, 0, 0))
    extra = () if below is None else (below,)
    return pl.pallas_call(
        final_kernel,
        grid=(steps,),
        in_specs=[
            pl.BlockSpec((1, 144, 384), lambda i: (i, 0, 0)),
            pl.BlockSpec((1, 144, 384), lambda i: (i + first, 0, 0)),
        ]
        + [sspec] * 4
        + [whole(up)]
        + [pl.BlockSpec(memory_space=pl.ANY)] * len(extra),
        out_specs=pl.BlockSpec((2, 24, 4608), lambda i: (i + first, 0, 0)),
        out_shape=jax.ShapeDtypeStruct((8, 24, 4608), BF),
        scratch_shapes=[pltpu.VMEM((3, 288, 128), F32)],
        input_output_aliases={7: 0} if extra else {},
        compiler_params=params(32),
        cost_estimate=pl.CostEstimate(flops=8 * 10**8, bytes_accessed=6 * 10**6, transcendentals=0),
    )(done_west, done_east, *quarters, up, *extra)


def passed_along(block, axis, distance):
    n = lax.axis_size(axis)
    return lax.ppermute(block, axis, [((i - distance) % n, i) for i in range(n)])


def packed_call(kernel, packed, shape, dtype):
    return pl.pallas_call(
        kernel,
        out_shape=jax.ShapeDtypeStruct(shape, dtype),
        in_specs=[pl.BlockSpec(memory_space=pltpu.VMEM)],
        out_specs=pl.BlockSpec(memory_space=pltpu.VMEM),
        compiler_params=pltpu.CompilerParams(vmem_limit_bytes=16 * MIB),
    )(packed)


def reduce_everywhere(packed, meanwhile):
    axes = ("lon", "lat")
    if lax.axis_size("lon") * lax.axis_size("lat") != packed.shape[0]:
        packed = lax.psum(packed.astype(F32), axes).astype(BF)
    else:
        parts = lax.all_to_all(packed, axes, 0, 0)
        parts, meanwhile = lax.optimization_barrier((parts, meanwhile))
        packed = lax.all_to_all(packed_call(sum_kernel, parts, packed.shape, BF), axes, 0, 0)
    return packed_call(unpack_kernel, packed, (384, 768), F32), meanwhile


def shards(
    field, cotangent,
    fine_gain_a, fine_qkv, fine_out, fine_bias, fine_gain_b, fine_in, fine_back,
    merge_gain, merge_weight,
    coarse_gain_a, coarse_qkv, coarse_out, coarse_bias, coarse_gain_b, coarse_in, coarse_back,
    up_weight,
):
    width = fine_qkv.shape[0]
    half = 6 * width
    halo = passed_along(field[:, :, :half], "lon", -1)
    cot_next = passed_along(cotangent[:, :, : 2 * half], "lon", -1)
    fine_consts = (
        fine_bias.reshape(fine_bias.shape[0], fine_bias.shape[1], 144, 144),
        fine_gain_a, fine_qkv, fine_out, fine_gain_b, fine_in, fine_back, merge_gain, merge_weight,
    )
    coarse_consts = (
        coarse_bias.reshape(coarse_bias.shape[0], coarse_bias.shape[1], 144, 144),
        coarse_gain_a, coarse_qkv, coarse_out, coarse_gain_b, coarse_in, coarse_back,
    )
    a_left, a_right, ca_left, ca_right = fine_call(field, 1, field, 2, fine_consts)
    ca_next = passed_along(ca_left, "lon", -1)
    b_left, b_right, cb_left, cb_right = fine_call(field, 3, halo, 0, fine_consts)
    b_prev = passed_along(b_right, "lon", 1)
    done_own, done_first, done_last, packed = coarse_call(
        (ca_right, cb_left, cb_right, ca_next), cotangent, cot_next, coarse_consts
    )
    first_prev = passed_along(done_first, "lon", 1)
    last_prev = passed_along(done_last, "lon", 1)
    packed, b_prev = lax.optimization_barrier((packed, b_prev))
    up_grad, first_prev = reduce_everywhere(packed, first_prev)
    quarters = (b_prev, a_left, a_right, b_left)
    output = final_call(0, first_prev, done_own, quarters, up_weight)
    output = final_call(done_first.shape[0], last_prev, done_own, quarters, up_weight, output)
    return output, up_grad


def solution(mesh):
    lat = P(None, "lat", None)
    split = P(None, "lat", "lon")
    return jax.shard_map(
        shards,
        mesh=mesh,
        in_specs=(split, split, P(), P(), P(), lat) + (P(),) * 8 + (lat,) + (P(),) * 4,
        out_specs=(split, P()),
        check_vma=False,
    )
```

time: 543 us -> 139 us (0.26); the launches traced: 534 us -> 138 us
  local copies, waits for them, and re-layouts: 177 us -> 12.8 us
  waiting for transfers between devices: 173 us -> 39.1 us
  matrix products: 106 us -> 0 us
  Pallas kernels: 0 us -> 54.3 us
  other arithmetic: 51 us -> 0 us
  starting transfers between devices: 10.9 us -> 31.2 us
  between operations: 14.5 us -> 0.77 us
    psum x1 -> x0, waiting for transfers between devices: 147 us -> none  [shards(): up_grad = lax.psum(local_grad, ('lon', 'lat'))]
    dot_general x27 -> x0, matrix products: 61.4 us -> none  [the longest x6 22 us: single(): jnp.einsum('nhqk,nkhd->nqhd', weights, packed[:, :, 2], preferred_element...]
    reshape x21 -> x2, local copies, waits for them, and re-layouts: 68 us -> 8.47 us  [the longest x1 4.34 us: shards(): coarse_bias.reshape(coarse_bias.shape[0], coarse_bias.shape[1], 144, 144)]
    pallas_call x0 -> x7, Pallas kernels: none -> 54.3 us  [the longest x2 30.7 us: fine_call(): pl.pallas_call(fine_kernel, grid=(steps,), in_specs=[spec(left_at), spec(...]
    sub x6 -> x0, matrix products: 45 us -> none  [single(): weights = jax.nn.softmax(scores, axis=-1).astype(jnp.bfloat16)]
    convert_element_type x20 -> x0, local copies, waits for them, and re-layouts: 35.9 us -> none  [the longest x2 12 us: merge_patches(): group_patches(value).astype(jnp.float32)]
    reduce_sum x20 -> x0, other arithmetic: 28.4 us -> none  [the longest x13 19 us: layer_norm(): spread = jnp.mean(center * center, axis=-1, keepdims=True)]
    all_to_all x0 -> x2, starting transfers between devices: none -> 17.6 us  [the longest x1 13.3 us: reduce_everywhere(): parts = lax.all_to_all(packed, axes, 0, 0)]
  transfers between devices with their start and end apart: 5 -> 8, of which waited for: 4 -> 3; matrix products, arithmetic and copies ran while one was open for 8% -> 7% of each run, Pallas kernels for 0% -> 38%
where the time goes in v1:
time: 139 us; the launch traced here: 138 us
  Pallas kernels  54.3 us (39%)
  waiting for transfers between devices  39.1 us (28%)
  starting transfers between devices  31.2 us (22%)
  local copies, waits for them, and re-layouts  12.8 us (9%)
    ppermute x6, waiting for transfers between devices, passed_along(): lax.ppermute(block, axis, [((i - distance) % n, i) for i in range(n)])  39.1 us
    pallas_call x2, Pallas kernels, fine_call(): pl.pallas_call(fine_kernel, grid=(steps,), in_specs=[spec(left_at), spec(...  30.7 us
    pallas_call x1, Pallas kernels, coarse_call(): pl.pallas_call(coarse_kernel, grid=(steps,), in_specs=[gspec] * 4 + [pl.B...  18.1 us
    ppermute x6, starting transfers between devices, passed_along(): lax.ppermute(block, axis, [((i - distance) % n, i) for i in range(n)])  13.6 us
    all_to_all x1, starting transfers between devices, reduce_everywhere(): parts = lax.all_to_all(packed, axes, 0, 0)  13.3 us
    reshape x1, local copies, waits for them, and re-layouts, shards(): coarse_bias.reshape(coarse_bias.shape[0], coarse_bias.shape[1], 144, 144)  4.34 us
    all_to_all x1, starting transfers between devices, reduce_everywhere(): lax.all_to_all(packed_call(sum_kernel, parts, packed.shape, BF), axes, 0, 0)  4.29 us
    reshape x1, local copies, waits for them, and re-layouts, shards(): fine_bias.reshape(fine_bias.shape[0], fine_bias.shape[1], 144, 144)  4.13 us
  transfers between devices with their start and end apart: 8, of which 3 were waited for; matrix products, arithmetic and copies ran while one was open for 7% of the time, Pallas kernels for 38%

profile of v1, /device:TPU:1, one launch (start us, length us, event | category | flops | bytes accessed | tf_op | source)
XLA Modules:
  0.0 138.3 jit_solution(9932706030745186960)
XLA Ops:
  0.6 0.0 copy-start.5
  0.6 1.3 slice.7
  2.0 9.6 %collective-permute-start.2 = (bf16[8,24,2304]{2,1,0:T(8,128)(2,1)S(1)}, bf16[8,24,2304]{2,1,0:T(8,128)(2,1)S(1)}, u32[]{:S(2)}, u32[]{:S(2)}) collective-permute-start(bf16[8,24,2304]{2,1,0:T(8,128)(2,1)S(1)} %slice.7), channel_id=1, source_target_pairs={{4,0},{8,4},{12,8},{16,12},{20,16},{24,20},{28,24},{32,28},{36,32}... | collective-permute-start | bytes 2654216 | tf_op jit(solution)/shard_map/ppermute | solution.py:401
  11.5 1.0 slice.6
  12.6 0.2 collective-permute-start
  12.8 0.0 copy-done.5
  12.8 4.1 %reshape.10.bias_ref = bf16[6,4,144,144]{3,2,1,0:T(8,128)(2,1)} reshape(bf16[6,4,20736]{2,1,0:T(4,128)(2,1)S(1)} %copy-done.5) | data formatting | bytes 1990656 | tf_op jit(solution)/shard_map/reshape | solution.py:437
  16.9 0.0 copy-start.6
  16.9 15.4 %shard_map.194 = (bf16[8,24,1152]{2,1,0:T(8,128)(2,1)}, bf16[8,24,1152]{2,1,0:T(8,128)(2,1)}, bf16[4,2,36,384]{3,2,1,0:T(8,128)(2,1)}, bf16[4,2,36,384]{3,2,1,0:T(8,128)(2,1)}) custom-call(bf16[8,24,4608]{2,1,0:T(8,128)(2,1)} %left_ref.3, bf16[8,24,4608]{2,1,0:T(8,128)(2,1)} %left_ref.3, bf16[6,4,144,144]{3,2,1,0:T(8,128)(2,1)} %reshape.10.bias_ref, ...), custom_call_target="tpu_custom_call" | custom-call | flops 3000000000 | bytes 6000000 | tf_op jit(solution)/shard_map/pallas_call | solution.py:330
  32.3 0.3 collective-permute-start.1
  32.6 0.0 copy-done.6
  32.6 4.3 %reshape.11.bias_ref = bf16[12,2,144,144]{3,2,1,0:T(8,128)(2,1)} reshape(bf16[12,2,20736]{2,1,0:T(2,128)(2,1)S(1)} %copy-done.6) | data formatting | bytes 1990656 | tf_op jit(solution)/shard_map/reshape | solution.py:441
  36.9 2.4 %collective-permute-done.right_ref = bf16[8,24,1152]{2,1,0:T(8,128)(2,1)} collective-permute-done((bf16[8,24,1152]{2,1,0:T(8,128)(2,1)S(1)}, bf16[8,24,1152]{2,1,0:T(8,128)(2,1)}, u32[]{:S(2)}, u32[]{:S(2)}) %collective-permute-start) | collective-permute-done | bytes 442400 | tf_op jit(solution)/shard_map/ppermute | solution.py:401
  39.3 15.3 %shard_map.195 = (bf16[8,24,1152]{2,1,0:T(8,128)(2,1)}, bf16[8,24,1152]{2,1,0:T(8,128)(2,1)}, bf16[4,2,36,384]{3,2,1,0:T(8,128)(2,1)}, bf16[4,2,36,384]{3,2,1,0:T(8,128)(2,1)}) custom-call(bf16[8,24,4608]{2,1,0:T(8,128)(2,1)} %left_ref.3, bf16[8,24,1152]{2,1,0:T(8,128)(2,1)} %collective-permute-done.right_ref, bf16[6,4,144,144]{3,2,1,0:T(8,128)(2,1)} %reshape.10.bias_ref, ...), custom_call_target="tpu_custom_call" | custom-call | flops 3000000000 | bytes 6000000 | tf_op jit(solution)/shard_map/pallas_call | solution.py:330
  54.7 0.3 collective-permute-start.4
  54.9 0.0 collective-permute-done.1.g3
  54.9 0.0 copy-start.8
  55.0 0.0 collective-permute-done.2.cot_next_ref
  55.0 0.0 copy-start.7
  55.0 0.7 copy-done.8
  55.7 0.3 copy-done.7
  55.9 18.1 %shard_map.196 = (bf16[4,144,384]{2,1,0:T(8,128)(2,1)}, bf16[2,144,384]{2,1,0:T(8,128)(2,1)}, bf16[2,144,384]{2,1,0:T(8,128)(2,1)}, bf16[128,18,128]{2,1,0:T(8,128)(2,1)}) custom-call(bf16[4,2,36,384]{3,2,1,0:T(8,128)(2,1)} %get-tuple-element.18.g0, bf16[4,2,36,384]{3,2,1,0:T(8,128)(2,1)} %get-tuple-element.19.g1, ...), custom_call_target="tpu_custom_call" | custom-call | flops 5000000000 | bytes 8000000 | tf_op jit(solution)/shard_map/pallas_call | solution.py:353
  74.1 0.0 collective-permute-done.4.set0
  74.1 13.3 %all-to-all-start = ((bf16[128,18,128]{2,1,0:T(8,128)(2,1)}), bf16[128,18,128]{2,1,0:T(8,128)(2,1)S(1)}, u32[]{:S(2)}, u32[]{:S(2)}) async-start(bf16[128,18,128]{2,1,0:T(8,128)(2,1)} %get-tuple-element.30), calls=%async_computation | async-start | bytes 1572864 | tf_op jit(solution)/shard_map/all_to_all | solution.py:419
  87.4 0.0 copy-start
  87.4 0.0 copy-start.1
  87.5 0.0 copy-start.2
  87.5 0.0 copy-start.3
  87.5 1.6 %collective-permute-start.5 = (bf16[2,144,384]{2,1,0:T(8,128)(2,1)}, bf16[2,144,384]{2,1,0:T(8,128)(2,1)S(1)}, u32[]{:S(2)}, u32[]{:S(2)}) collective-permute-start(bf16[2,144,384]{2,1,0:T(8,128)(2,1)} %get-tuple-element.31), channel_id=1, source_target_pairs={{124,0},{0,4},{4,8},{8,12},{12,16},{16,20},{20,24},{24,28},{28,32}... | collective-permute-start | bytes 663560 | tf_op jit(solution)/shard_map/ppermute | solution.py:401
  89.1 19.7 %collective-permute-done.5.done_west = bf16[2,144,384]{2,1,0:T(8,128)(2,1)S(1)} collective-permute-done((bf16[2,144,384]{2,1,0:T(8,128)(2,1)}, bf16[2,144,384]{2,1,0:T(8,128)(2,1)S(1)}, u32[]{:S(2)}, u32[]{:S(2)}) %collective-permute-start.5) | collective-permute-done | bytes 221216 | tf_op jit(solution)/shard_map/ppermute | solution.py:401
  108.7 0.0 all-to-all-done.in_ref
  108.7 1.1 shard_map.199
  109.8 4.3 %all-to-all-start.1 = ((bf16[128,18,128]{2,1,0:T(8,128)(2,1)}), bf16[128,18,128]{2,1,0:T(8,128)(2,1)S(1)}, u32[]{:S(2)}, u32[]{:S(2)}) async-start(bf16[128,18,128]{2,1,0:T(8,128)(2,1)} %shard_map.199), calls=%async_computation.1 | async-start | bytes 1572864 | tf_op jit(solution)/shard_map/all_to_all | solution.py:421
  114.1 1.7 %collective-permute-start.3 = (bf16[2,144,384]{2,1,0:T(8,128)(2,1)}, bf16[2,144,384]{2,1,0:T(8,128)(2,1)S(1)}, u32[]{:S(2)}, u32[]{:S(2)}) collective-permute-start(bf16[2,144,384]{2,1,0:T(8,128)(2,1)} %get-tuple-element.22), channel_id=1, source_target_pairs={{124,0},{0,4},{4,8},{8,12},{12,16},{16,20},{20,24},{24,28},{28,32}... | collective-permute-start | bytes 663560 | tf_op jit(solution)/shard_map/ppermute | solution.py:401
  115.8 0.0 copy-done
  115.8 0.0 copy-done.1
  115.8 0.0 copy-done.2
  115.8 0.0 copy-done.3
  115.9 0.0 copy-start.4
  115.9 1.0 copy-done.4
  116.9 1.6 %shard_map.197.rest_0_ = bf16[8,24,4608]{2,1,0:T(8,128)(2,1)} custom-call(bf16[2,144,384]{2,1,0:T(8,128)(2,1)S(1)} %collective-permute-done.5.done_west, bf16[4,144,384]{2,1,0:T(8,128)(2,1)S(1)} %copy-done.4, bf16[8,24,1152]{2,1,0:T(8,128)(2,1)S(1)} %collective-permute-done.4.set0, bf16[8,24,1152]{2,1,0:T(8,128)(2,1)S(1)} %copy-done.1, ...), custom_call_target="tpu_custom_call" | custom-call | flops 800000000 | bytes 6000000 | tf_op jit(solution)/shard_map/pallas_call | solution.py:380
  118.5 17.1 %collective-permute-done.3.done_west = bf16[2,144,384]{2,1,0:T(8,128)(2,1)S(1)} collective-permute-done((bf16[2,144,384]{2,1,0:T(8,128)(2,1)}, bf16[2,144,384]{2,1,0:T(8,128)(2,1)S(1)}, u32[]{:S(2)}, u32[]{:S(2)}) %collective-permute-start.3) | collective-permute-done | bytes 221216 | tf_op jit(solution)/shard_map/ppermute | solution.py:401
  135.5 1.6 %shard_map.198 = bf16[8,24,4608]{2,1,0:T(8,128)(2,1)} custom-call(bf16[2,144,384]{2,1,0:T(8,128)(2,1)S(1)} %collective-permute-done.3.done_west, bf16[4,144,384]{2,1,0:T(8,128)(2,1)S(1)} %copy-done.4, bf16[8,24,1152]{2,1,0:T(8,128)(2,1)S(1)} %collective-permute-done.4.set0, bf16[8,24,1152]{2,1,0:T(8,128)(2,1)S(1)} %copy-done.1, ...), custom_call_target="tpu_custom_call", output_to_operand_aliasing={{}: (7, {})} | custom-call | flops 800000000 | bytes 6000000 | tf_op jit(solution)/shard_map/pallas_call | solution.py:380
  137.2 0.0 all-to-all-done.1.in_ref
  137.2 1.1 shard_map.200
Async XLA Ops:
  0.6 12.1 %copy-start.5 = (bf16[6,4,20736]{2,1,0:T(4,128)(2,1)S(1)}, bf16[6,4,20736]{2,1,0:T(4,128)(2,1)}, u32[]{:S(2)}) copy-start(bf16[6,4,20736]{2,1,0:T(4,128)(2,1)} %param.24) | copy-start | bytes 2985988
  2.0 53.0 %collective-permute-start.2 = (bf16[8,24,2304]{2,1,0:T(8,128)(2,1)S(1)}, bf16[8,24,2304]{2,1,0:T(8,128)(2,1)S(1)}, u32[]{:S(2)}, u32[]{:S(2)}) collective-permute-start(bf16[8,24,2304]{2,1,0:T(8,128)(2,1)S(1)} %slice.7), channel_id=1, source_target_pairs={{4,0},{8,4},{12,8},{16,12},{20,16},{24,20},{28,24},{32,28},{36,32}... | collective-permute-start | bytes 2654216 | tf_op jit(solution)/shard_map/ppermute | solution.py:401
  12.6 26.7 %collective-permute-start = (bf16[8,24,1152]{2,1,0:T(8,128)(2,1)S(1)}, bf16[8,24,1152]{2,1,0:T(8,128)(2,1)}, u32[]{:S(2)}, u32[]{:S(2)}) collective-permute-start(bf16[8,24,1152]{2,1,0:T(8,128)(2,1)S(1)} %slice.6), channel_id=1, source_target_pairs={{4,0},{8,4},{12,8},{16,12},{20,16},{24,20},{28,24},{32,28},{36,32}... | collective-permute-start | bytes 1327112 | tf_op jit(solution)/shard_map/ppermute | solution.py:401
  16.9 15.7 %copy-start.6 = (bf16[12,2,20736]{2,1,0:T(2,128)(2,1)S(1)}, bf16[12,2,20736]{2,1,0:T(2,128)(2,1)}, u32[]{:S(2)}) copy-start(bf16[12,2,20736]{2,1,0:T(2,128)(2,1)} %param.33) | copy-start | bytes 2985988
  32.3 22.6 %collective-permute-start.1 = (bf16[4,2,36,384]{3,2,1,0:T(8,128)(2,1)}, bf16[4,2,36,384]{3,2,1,0:T(8,128)(2,1)S(1)}, u32[]{:S(2)}, u32[]{:S(2)}) collective-permute-start(bf16[4,2,36,384]{3,2,1,0:T(8,128)(2,1)} %get-tuple-element.21), channel_id=1, source_target_pairs={{4,0},{8,4},{12,8},{16,12},{20,16},{24,20},{28,24},{32,28},{36,32}... | collective-permute-start | bytes 663560 | tf_op jit(solution)/shard_map/ppermute | solution.py:401
  54.7 19.4 %collective-permute-start.4 = (bf16[8,24,1152]{2,1,0:T(8,128)(2,1)}, bf16[8,24,1152]{2,1,0:T(8,128)(2,1)S(1)}, u32[]{:S(2)}, u32[]{:S(2)}) collective-permute-start(bf16[8,24,1152]{2,1,0:T(8,128)(2,1)} %get-tuple-element.25), channel_id=1, source_target_pairs={{124,0},{0,4},{4,8},{8,12},{12,16},{16,20},{20,24},{24,28},{28,32}... | collective-permute-start | bytes 1327112 | tf_op jit(solution)/shard_map/ppermute | solution.py:401
  54.9 0.7 copy-start.8
  55.0 1.0 copy-start.7
  74.1 34.6 %all-to-all-start = ((bf16[128,18,128]{2,1,0:T(8,128)(2,1)}), bf16[128,18,128]{2,1,0:T(8,128)(2,1)S(1)}, u32[]{:S(2)}, u32[]{:S(2)}) async-start(bf16[128,18,128]{2,1,0:T(8,128)(2,1)} %get-tuple-element.30), calls=%async_computation | async-start | bytes 1572864 | tf_op jit(solution)/shard_map/all_to_all | solution.py:419
  87.4 28.4 %copy-start = (bf16[384,768]{1,0:T(8,128)(2,1)S(1)}, bf16[384,768]{1,0:T(8,128)(2,1)}, u32[]{:S(2)}) copy-start(bf16[384,768]{1,0:T(8,128)(2,1)} %up_ref.3) | copy-start | bytes 1769476
  87.4 28.4 %copy-start.1 = (bf16[8,24,1152]{2,1,0:T(8,128)(2,1)S(1)}, bf16[8,24,1152]{2,1,0:T(8,128)(2,1)}, u32[]{:S(2)}) copy-start(bf16[8,24,1152]{2,1,0:T(8,128)(2,1)} %get-tuple-element.27.set1) | copy-start | bytes 1327108
  87.5 28.4 %copy-start.2 = (bf16[8,24,1152]{2,1,0:T(8,128)(2,1)S(1)}, bf16[8,24,1152]{2,1,0:T(8,128)(2,1)}, u32[]{:S(2)}) copy-start(bf16[8,24,1152]{2,1,0:T(8,128)(2,1)} %get-tuple-element.28.set2) | copy-start | bytes 1327108
  87.5 28.4 %copy-start.3 = (bf16[8,24,1152]{2,1,0:T(8,128)(2,1)S(1)}, bf16[8,24,1152]{2,1,0:T(8,128)(2,1)}, u32[]{:S(2)}) copy-start(bf16[8,24,1152]{2,1,0:T(8,128)(2,1)} %get-tuple-element.29.set3) | copy-start | bytes 1327108
  87.5 21.2 %collective-permute-start.5 = (bf16[2,144,384]{2,1,0:T(8,128)(2,1)}, bf16[2,144,384]{2,1,0:T(8,128)(2,1)S(1)}, u32[]{:S(2)}, u32[]{:S(2)}) collective-permute-start(bf16[2,144,384]{2,1,0:T(8,128)(2,1)} %get-tuple-element.31), channel_id=1, source_target_pairs={{124,0},{0,4},{4,8},{8,12},{12,16},{16,20},{20,24},{24,28},{28,32}... | collective-permute-start | bytes 663560 | tf_op jit(solution)/shard_map/ppermute | solution.py:401
  109.8 27.3 %all-to-all-start.1 = ((bf16[128,18,128]{2,1,0:T(8,128)(2,1)}), bf16[128,18,128]{2,1,0:T(8,128)(2,1)S(1)}, u32[]{:S(2)}, u32[]{:S(2)}) async-start(bf16[128,18,128]{2,1,0:T(8,128)(2,1)} %shard_map.199), calls=%async_computation.1 | async-start | bytes 1572864 | tf_op jit(solution)/shard_map/all_to_all | solution.py:421
  114.1 21.4 %collective-permute-start.3 = (bf16[2,144,384]{2,1,0:T(8,128)(2,1)}, bf16[2,144,384]{2,1,0:T(8,128)(2,1)S(1)}, u32[]{:S(2)}, u32[]{:S(2)}) collective-permute-start(bf16[2,144,384]{2,1,0:T(8,128)(2,1)} %get-tuple-element.22), channel_id=1, source_target_pairs={{124,0},{0,4},{4,8},{8,12},{12,16},{16,20},{20,24},{24,28},{28,32}... | collective-permute-start | bytes 663560 | tf_op jit(solution)/shard_map/ppermute | solution.py:401
  115.9 1.0 copy-start.4

commit v2 on v1

--- a/solution.py
+++ b/solution.py
@@ -209,7 +209,7 @@
 def coarse_kernel(
     g0, g1, g2, g3, cot_ref, cot_next_ref, bias_ref, ga_ref, wqkv_ref, wo_ref, gb_ref,
     wi_ref, wb_ref,
-    done_own, done_first, done_last, packed_ref, nat_ref, win_ref, table_ref, mixed_ref, grad_ref,
+    done_own, done_next, packed_ref, nat_ref, win_ref, table_ref, mixed_ref, grad_ref,
 ):
     heads = bias_ref.shape[0]
 
@@ -223,16 +223,12 @@
         [
             coarse_unit(
                 u, (g0, g1, g2, g3), cot_ref, cot_next_ref, ga_ref, wqkv_ref, wo_ref, gb_ref, wi_ref, wb_ref,
-                done_own, done_last, grad_ref, nat_ref.at[u], win_ref.at[u], table_ref, mixed_ref.at[u],
+                done_own, done_next, grad_ref, nat_ref.at[u], win_ref.at[u], table_ref, mixed_ref.at[u],
             )
             for u in range(units)
         ],
         LEAD if units > 1 else 0,
     )
-
-    @pl.when(pl.program_id(0) == 0)
-    def _():
-        done_first[...] = done_last[...]
 
     @pl.when(pl.program_id(0) == pl.num_programs(0) - 1)
     def _():
@@ -295,8 +291,7 @@
         yield
 
 
-def final_kernel(done_west, done_east, set0, set1, set2, set3, up_ref, *rest):
-    out_ref, rows_ref = rest[-2:]
+def final_kernel(done_west, done_east, set0, set1, set2, set3, up_ref, out_ref, rows_ref):
     width = done_west.shape[2]
     halves = (set0, set1, set2, set3)
     for e, done_ref in enumerate((done_west, done_east)):
@@ -356,10 +351,8 @@
         in_specs=[gspec] * 4
         + [pl.BlockSpec((2 * UNITS, 24, 2304), lambda i: (i, 0, 1)), pl.BlockSpec((2 * UNITS, 24, 2304), lambda i: (i, 0, 0))]
         + [whole(c) for c in consts],
-        out_specs=[dspec] + [pl.BlockSpec((UNITS, 144, 384), lambda i: (0, 0, 0))] * 2
-        + [pl.BlockSpec((128, 18, 128), lambda i: (0, 0, 0))],
-        out_shape=[jax.ShapeDtypeStruct((steps * UNITS, 144, 384), BF)]
-        + [jax.ShapeDtypeStruct((UNITS, 144, 384), BF)] * 2
+        out_specs=[dspec, dspec, pl.BlockSpec((128, 18, 128), lambda i: (0, 0, 0))],
+        out_shape=[jax.ShapeDtypeStruct((steps * UNITS, 144, 384), BF)] * 2
         + [jax.ShapeDtypeStruct((128, 18, 128), BF)],
         scratch_shapes=[
             pltpu.VMEM((UNITS, 3, 288, 128), F32),
@@ -373,27 +366,20 @@
     )(*groups, cot, cot_next, *consts)
 
 
-def final_call(first, done_west, done_east, quarters, up, below=None):
+def final_call(done_west, done_east, quarters, up):
     steps = done_west.shape[0]
-    sspec = pl.BlockSpec((2, 24, 1152), lambda i: (i + first, 0, 0))
-    extra = () if below is None else (below,)
+    dspec = pl.BlockSpec((1, 144, 384), lambda i: (i, 0, 0))
+    sspec = pl.BlockSpec((2, 24, 1152), lambda i: (i, 0, 0))
     return pl.pallas_call(
         final_kernel,
         grid=(steps,),
-        in_specs=[
-            pl.BlockSpec((1, 144, 384), lambda i: (i, 0, 0)),
-            pl.BlockSpec((1, 144, 384), lambda i: (i + first, 0, 0)),
-        ]
-        + [sspec] * 4
-        + [whole(up)]
-        + [pl.BlockSpec(memory_space=pl.ANY)] * len(extra),
-        out_specs=pl.BlockSpec((2, 24, 4608), lambda i: (i + first, 0, 0)),
-        out_shape=jax.ShapeDtypeStruct((8, 24, 4608), BF),
+        in_specs=[dspec] * 2 + [sspec] * 4 + [whole(up)],
+        out_specs=pl.BlockSpec((2, 24, 4608), lambda i: (i, 0, 0)),
+        out_shape=jax.ShapeDtypeStruct((2 * steps, 24, 4608), BF),
         scratch_shapes=[pltpu.VMEM((3, 288, 128), F32)],
-        input_output_aliases={7: 0} if extra else {},
         compiler_params=params(32),
-        cost_estimate=pl.CostEstimate(flops=8 * 10**8, bytes_accessed=6 * 10**6, transcendentals=0),
-    )(done_west, done_east, *quarters, up, *extra)
+        cost_estimate=pl.CostEstimate(flops=10**11, bytes_accessed=6 * 10**6, transcendentals=0),
+    )(done_west, done_east, *quarters, up)
 
 
 def passed_along(block, axis, distance):
@@ -432,7 +418,6 @@
     width = fine_qkv.shape[0]
     half = 6 * width
     halo = passed_along(field[:, :, :half], "lon", -1)
-    cot_next = passed_along(cotangent[:, :, : 2 * half], "lon", -1)
     fine_consts = (
         fine_bias.reshape(fine_bias.shape[0], fine_bias.shape[1], 144, 144),
         fine_gain_a, fine_qkv, fine_out, fine_gain_b, fine_in, fine_back, merge_gain, merge_weight,
@@ -442,19 +427,17 @@
         coarse_gain_a, coarse_qkv, coarse_out, coarse_gain_b, coarse_in, coarse_back,
     )
     a_left, a_right, ca_left, ca_right = fine_call(field, 1, field, 2, fine_consts)
+    halo, ca_left, a_left = lax.optimization_barrier((halo, ca_left, a_left))
     ca_next = passed_along(ca_left, "lon", -1)
+    cot_first, a_left = lax.optimization_barrier((cotangent[:, :, : 2 * half], a_left))
+    cot_next = passed_along(cot_first, "lon", -1)
     b_left, b_right, cb_left, cb_right = fine_call(field, 3, halo, 0, fine_consts)
     b_prev = passed_along(b_right, "lon", 1)
-    done_own, done_first, done_last, packed = coarse_call(
-        (ca_right, cb_left, cb_right, ca_next), cotangent, cot_next, coarse_consts
-    )
-    first_prev = passed_along(done_first, "lon", 1)
-    last_prev = passed_along(done_last, "lon", 1)
+    done_own, done_next, packed = coarse_call((ca_right, cb_left, cb_right, ca_next), cotangent, cot_next, coarse_consts)
+    done_prev = passed_along(done_next, "lon", 1)
     packed, b_prev = lax.optimization_barrier((packed, b_prev))
-    up_grad, first_prev = reduce_everywhere(packed, first_prev)
-    quarters = (b_prev, a_left, a_right, b_left)
-    output = final_call(0, first_prev, done_own, quarters, up_weight)
-    output = final_call(done_first.shape[0], last_prev, done_own, quarters, up_weight, output)
+    output = final_call(done_prev, done_own, (b_prev, a_left, a_right, b_left), up_weight)
+    up_grad, output = reduce_everywhere(packed, output)
     return output, up_grad
 
 

time: 139 us -> 126 us (0.906)
  waiting for transfers between devices: 39.1 us -> 15.7 us
  blocking collectives: 0 us -> 20.3 us
  starting transfers between devices: 31.2 us -> 22 us
    ppermute x6 -> x5, waiting for transfers between devices: 39.1 us -> 9.29 us  [passed_along(): lax.ppermute(block, axis, [((i - distance) % n, i) for i in range(n)])]
    all_to_all x0 -> x1, blocking collectives: none -> 20.3 us  [reduce_everywhere(): lax.all_to_all(packed_call(sum_kernel, parts, packed.shape, BF), axes, 0, 0)]
    all_to_all x1, waiting for transfers between devices: 0.01 us -> 6.39 us  [reduce_everywhere(): parts = lax.all_to_all(packed, axes, 0, 0)]
    all_to_all x1 -> x0, starting transfers between devices: 4.29 us -> none  [reduce_everywhere(): lax.all_to_all(packed_call(sum_kernel, parts, packed.shape, BF), axes, 0, 0)]
    all_to_all x1, starting transfers between devices: 13.3 us -> 10.5 us  [reduce_everywhere(): parts = lax.all_to_all(packed, axes, 0, 0)]
    ppermute x6 -> x5, starting transfers between devices: 13.6 us -> 11.6 us  [passed_along(): lax.ppermute(block, axis, [((i - distance) % n, i) for i in range(n)])]
    unnamed x18 -> x22, local copies, waits for them, and re-layouts: 2 us -> 3.04 us
    pallas_call x2 -> x1, Pallas kernels: 3.24 us -> 2.8 us  [final_call(): pl.pallas_call(final_kernel, grid=(steps,), in_specs=[dspec] * 2 + [sspec...]
  transfers between devices with their start and end apart: 8 -> 6, of which waited for: 3 -> 3; matrix products, arithmetic and copies ran while one was open for 7% -> 8% of each run, Pallas kernels for 38% -> 41%
where the time goes in v2:
time: 126 us
  Pallas kernels  53 us (42%)
  starting transfers between devices  22 us (17%)
  blocking collectives  20.3 us (16%)
  waiting for transfers between devices  15.7 us (12%)
  local copies, waits for them, and re-layouts  13.9 us (11%)
    pallas_call x2, Pallas kernels, fine_call(): pl.pallas_call(fine_kernel, grid=(steps,), in_specs=[spec(left_at), spec(...  30.8 us
    all_to_all x1, blocking collectives, reduce_everywhere(): lax.all_to_all(packed_call(sum_kernel, parts, packed.shape, BF), axes, 0, 0)  20.3 us
    pallas_call x1, Pallas kernels, coarse_call(): pl.pallas_call(coarse_kernel, grid=(steps,), in_specs=[gspec] * 4 + [pl.B...  18.1 us
    ppermute x5, starting transfers between devices, passed_along(): lax.ppermute(block, axis, [((i - distance) % n, i) for i in range(n)])  11.6 us
    all_to_all x1, starting transfers between devices, reduce_everywhere(): parts = lax.all_to_all(packed, axes, 0, 0)  10.5 us
    ppermute x5, waiting for transfers between devices, passed_along(): lax.ppermute(block, axis, [((i - distance) % n, i) for i in range(n)])  9.29 us
    all_to_all x1, waiting for transfers between devices, reduce_everywhere(): parts = lax.all_to_all(packed, axes, 0, 0)  6.39 us
    reshape x1, local copies, waits for them, and re-layouts, shards(): coarse_bias.reshape(coarse_bias.shape[0], coarse_bias.shape[1], 144, 144)  4.36 us
  transfers between devices with their start and end apart: 6, of which 3 were waited for; matrix products, arithmetic and copies ran while one was open for 8% of the time, Pallas kernels for 41%

profile of v2, /device:TPU:1, one launch (start us, length us, event | category | flops | bytes accessed | tf_op | source)
XLA Modules:
  0.0 125.7 jit_solution(6797831215434819319)
XLA Ops:
  0.6 0.0 copy-start.5
  0.6 1.1 slice.6
  1.8 9.6 %collective-permute-start = (bf16[8,24,1152]{2,1,0:T(8,128)(2,1)S(1)}, bf16[8,24,1152]{2,1,0:T(8,128)(2,1)S(1)}, u32[]{:S(2)}, u32[]{:S(2)}) collective-permute-start(bf16[8,24,1152]{2,1,0:T(8,128)(2,1)S(1)} %slice.6), channel_id=1, source_target_pairs={{4,0},{8,4},{12,8},{16,12},{20,16},{24,20},{28,24},{32,28},{36,32}... | collective-permute-start | bytes 1327112 | tf_op jit(solution)/shard_map/ppermute | solution.py:387
  11.3 1.2 slice.7
  12.6 0.0 copy-done.5
  12.6 4.2 %reshape.10.bias_ref = bf16[6,4,144,144]{3,2,1,0:T(8,128)(2,1)} reshape(bf16[6,4,20736]{2,1,0:T(4,128)(2,1)S(1)} %copy-done.5) | data formatting | bytes 1990656 | tf_op jit(solution)/shard_map/reshape | solution.py:422
  16.7 0.0 copy-start.6
  16.7 15.4 %shard_map.194 = (bf16[8,24,1152]{2,1,0:T(8,128)(2,1)}, bf16[8,24,1152]{2,1,0:T(8,128)(2,1)}, bf16[4,2,36,384]{3,2,1,0:T(8,128)(2,1)}, bf16[4,2,36,384]{3,2,1,0:T(8,128)(2,1)}) custom-call(bf16[8,24,4608]{2,1,0:T(8,128)(2,1)} %left_ref.3, bf16[8,24,4608]{2,1,0:T(8,128)(2,1)} %left_ref.3, bf16[6,4,144,144]{3,2,1,0:T(8,128)(2,1)} %reshape.10.bias_ref, ...), custom_call_target="tpu_custom_call" | custom-call | flops 3000000000 | bytes 6000000 | tf_op jit(solution)/shard_map/pallas_call | solution.py:325
  32.1 0.0 copy-start.9
  32.2 0.0 collective-permute-done.right_ref
  32.2 0.0 copy-start.8
  32.2 0.2 collective-permute-start.2
  32.4 0.0 copy-done.6
  32.4 4.4 %reshape.11.bias_ref = bf16[12,2,144,144]{3,2,1,0:T(8,128)(2,1)} reshape(bf16[12,2,20736]{2,1,0:T(2,128)(2,1)S(1)} %copy-done.6) | data formatting | bytes 1990656 | tf_op jit(solution)/shard_map/reshape | solution.py:426
  36.7 0.0 copy-done.9
  36.7 0.0 collective-permute-start.1
  36.8 0.0 copy-done.8
  36.8 15.4 %shard_map.195 = (bf16[8,24,1152]{2,1,0:T(8,128)(2,1)}, bf16[8,24,1152]{2,1,0:T(8,128)(2,1)}, bf16[4,2,36,384]{3,2,1,0:T(8,128)(2,1)}, bf16[4,2,36,384]{3,2,1,0:T(8,128)(2,1)}) custom-call(bf16[8,24,4608]{2,1,0:T(8,128)(2,1)} %left_ref.3, bf16[8,24,1152]{2,1,0:T(8,128)(2,1)} %copy-done.8, bf16[6,4,144,144]{3,2,1,0:T(8,128)(2,1)} %reshape.10.bias_ref, ...), custom_call_target="tpu_custom_call" | custom-call | flops 3000000000 | bytes 6000000 | tf_op jit(solution)/shard_map/pallas_call | solution.py:325
  52.1 1.7 %collective-permute-start.3 = (bf16[8,24,1152]{2,1,0:T(8,128)(2,1)}, bf16[8,24,1152]{2,1,0:T(8,128)(2,1)S(1)}, u32[]{:S(2)}, u32[]{:S(2)}) collective-permute-start(bf16[8,24,1152]{2,1,0:T(8,128)(2,1)} %get-tuple-element.32), channel_id=1, source_target_pairs={{124,0},{0,4},{4,8},{8,12},{12,16},{16,20},{20,24},{24,28},{28,32}... | collective-permute-start | bytes 1327112 | tf_op jit(solution)/shard_map/ppermute | solution.py:387
  53.8 3.9 %collective-permute-done.1.g3 = bf16[4,2,36,384]{3,2,1,0:T(8,128)(2,1)S(1)} collective-permute-done((bf16[4,2,36,384]{3,2,1,0:T(8,128)(2,1)S(1)}, bf16[4,2,36,384]{3,2,1,0:T(8,128)(2,1)S(1)}, u32[]{:S(2)}, u32[]{:S(2)}) %collective-permute-start.1) | collective-permute-done | bytes 221216 | tf_op jit(solution)/shard_map/ppermute | solution.py:387
  57.7 0.0 copy-start.10
  57.7 0.0 collective-permute-done.2.cot_next_ref
  57.7 0.0 copy-start.7
  57.7 0.7 copy-done.10
  58.4 0.3 copy-done.7
  58.7 0.0 copy-start
  58.7 0.0 copy-start.1
  58.7 0.0 copy-start.2
  58.7 18.1 %shard_map.196 = (bf16[4,144,384]{2,1,0:T(8,128)(2,1)}, bf16[4,144,384]{2,1,0:T(8,128)(2,1)}, bf16[128,18,128]{2,1,0:T(8,128)(2,1)}) custom-call(bf16[4,2,36,384]{3,2,1,0:T(8,128)(2,1)} %get-tuple-element.22.g0, bf16[4,2,36,384]{3,2,1,0:T(8,128)(2,1)} %get-tuple-element.26.g1, bf16[4,2,36,384]{3,2,1,0:T(8,128)(2,1)} %get-tuple-element.27.g2, ...), custom_call_target="tpu_custom_call" | custom-call | flops 5000000000 | bytes 8000000 | tf_op jit(solution)/shard_map/pallas_call | solution.py:348
  76.8 0.1 collective-permute-start.4
  76.9 0.0 collective-permute-done.3.set0
  76.9 10.5 %all-to-all-start = ((bf16[128,18,128]{2,1,0:T(8,128)(2,1)}), bf16[128,18,128]{2,1,0:T(8,128)(2,1)S(1)}, u32[]{:S(2)}, u32[]{:S(2)}) async-start(bf16[128,18,128]{2,1,0:T(8,128)(2,1)} %get-tuple-element.33), calls=%async_computation | async-start | bytes 1572864 | tf_op jit(solution)/shard_map/all_to_all | solution.py:405
  87.4 5.4 %collective-permute-done.4.done_west = bf16[4,144,384]{2,1,0:T(8,128)(2,1)S(1)} collective-permute-done((bf16[4,144,384]{2,1,0:T(8,128)(2,1)}, bf16[4,144,384]{2,1,0:T(8,128)(2,1)S(1)}, u32[]{:S(2)}, u32[]{:S(2)}) %collective-permute-start.4) | collective-permute-done | bytes 442400 | tf_op jit(solution)/shard_map/ppermute | solution.py:387
  92.8 0.0 copy-done
  92.8 0.0 copy-done.1
  92.8 0.0 copy-done.2
  92.8 0.0 copy-start.3
  92.8 1.0 copy-done.3
  93.8 0.0 copy-start.4
  93.8 1.0 copy-done.4
  94.9 2.8 %shard_map.197 = bf16[8,24,4608]{2,1,0:T(8,128)(2,1)} custom-call(bf16[4,144,384]{2,1,0:T(8,128)(2,1)S(1)} %collective-permute-done.4.done_west, bf16[4,144,384]{2,1,0:T(8,128)(2,1)S(1)} %copy-done.4, bf16[8,24,1152]{2,1,0:T(8,128)(2,1)S(1)} %collective-permute-done.3.set0, bf16[8,24,1152]{2,1,0:T(8,128)(2,1)S(1)} %copy-done.1, ...), custom_call_target="tpu_custom_call" | custom-call | flops 99999997952 | bytes 6000000 | tf_op jit(solution)/shard_map/pallas_call | solution.py:373
  97.7 6.4 %all-to-all-done.in_ref = bf16[128,18,128]{2,1,0:T(8,128)(2,1)S(1)} async-done(((bf16[128,18,128]{2,1,0:T(8,128)(2,1)}), bf16[128,18,128]{2,1,0:T(8,128)(2,1)S(1)}, u32[]{:S(2)}, u32[]{:S(2)}) %all-to-all-start) | async-done | bytes 589856 | tf_op jit(solution)/shard_map/all_to_all | solution.py:405
  104.0 0.2 shard_map.198
  104.3 20.3 %all_to_all.10.in_ref = bf16[128,18,128]{2,1,0:T(8,128)(2,1)S(1)} all-to-all(bf16[128,18,128]{2,1,0:T(8,128)(2,1)S(1)} %shard_map.198), channel_id=1, replica_groups=mesh['lon'=32,'lat'=4] {'lon','lat'}, dimensions={0} | all-to-all | bytes 1179648 | tf_op jit(solution)/shard_map/all_to_all | solution.py:407
  124.6 1.1 shard_map.199
Async XLA Ops:
  0.6 11.9 %copy-start.5 = (bf16[6,4,20736]{2,1,0:T(4,128)(2,1)S(1)}, bf16[6,4,20736]{2,1,0:T(4,128)(2,1)}, u32[]{:S(2)}) copy-start(bf16[6,4,20736]{2,1,0:T(4,128)(2,1)} %param.24) | copy-start | bytes 2985988
  1.8 30.4 %collective-permute-start = (bf16[8,24,1152]{2,1,0:T(8,128)(2,1)S(1)}, bf16[8,24,1152]{2,1,0:T(8,128)(2,1)S(1)}, u32[]{:S(2)}, u32[]{:S(2)}) collective-permute-start(bf16[8,24,1152]{2,1,0:T(8,128)(2,1)S(1)} %slice.6), channel_id=1, source_target_pairs={{4,0},{8,4},{12,8},{16,12},{20,16},{24,20},{28,24},{32,28},{36,32}... | collective-permute-start | bytes 1327112 | tf_op jit(solution)/shard_map/ppermute | solution.py:387
  16.7 15.6 %copy-start.6 = (bf16[12,2,20736]{2,1,0:T(2,128)(2,1)S(1)}, bf16[12,2,20736]{2,1,0:T(2,128)(2,1)}, u32[]{:S(2)}) copy-start(bf16[12,2,20736]{2,1,0:T(2,128)(2,1)} %param.33) | copy-start | bytes 2985988
  32.1 4.6 %copy-start.9 = (bf16[4,2,36,384]{3,2,1,0:T(8,128)(2,1)S(1)}, bf16[4,2,36,384]{3,2,1,0:T(8,128)(2,1)}, u32[]{:S(2)}) copy-start(bf16[4,2,36,384]{3,2,1,0:T(8,128)(2,1)} %get-tuple-element.28) | copy-start | bytes 663556
  32.2 4.6 %copy-start.8 = (bf16[8,24,1152]{2,1,0:T(8,128)(2,1)}, bf16[8,24,1152]{2,1,0:T(8,128)(2,1)S(1)}, u32[]{:S(2)}) copy-start(bf16[8,24,1152]{2,1,0:T(8,128)(2,1)S(1)} %collective-permute-done.right_ref) | copy-start | bytes 1327108
  32.2 25.5 %collective-permute-start.2 = (bf16[8,24,2304]{2,1,0:T(8,128)(2,1)S(1)}, bf16[8,24,2304]{2,1,0:T(8,128)(2,1)S(1)}, u32[]{:S(2)}, u32[]{:S(2)}) collective-permute-start(bf16[8,24,2304]{2,1,0:T(8,128)(2,1)S(1)} %slice.7), channel_id=1, source_target_pairs={{4,0},{8,4},{12,8},{16,12},{20,16},{24,20},{28,24},{32,28},{36,32}... | collective-permute-start | bytes 2654216 | tf_op jit(solution)/shard_map/ppermute | solution.py:387
  36.7 21.0 %collective-permute-start.1 = (bf16[4,2,36,384]{3,2,1,0:T(8,128)(2,1)S(1)}, bf16[4,2,36,384]{3,2,1,0:T(8,128)(2,1)S(1)}, u32[]{:S(2)}, u32[]{:S(2)}) collective-permute-start(bf16[4,2,36,384]{3,2,1,0:T(8,128)(2,1)S(1)} %copy-done.9), channel_id=1, source_target_pairs={{4,0},{8,4},{12,8},{16,12},{20,16},{24,20},{28,24},{32,28},{36,32}... | collective-permute-start | bytes 663560 | tf_op jit(solution)/shard_map/ppermute | solution.py:387
  52.1 24.8 %collective-permute-start.3 = (bf16[8,24,1152]{2,1,0:T(8,128)(2,1)}, bf16[8,24,1152]{2,1,0:T(8,128)(2,1)S(1)}, u32[]{:S(2)}, u32[]{:S(2)}) collective-permute-start(bf16[8,24,1152]{2,1,0:T(8,128)(2,1)} %get-tuple-element.32), channel_id=1, source_target_pairs={{124,0},{0,4},{4,8},{8,12},{12,16},{16,20},{20,24},{24,28},{28,32}... | collective-permute-start | bytes 1327112 | tf_op jit(solution)/shard_map/ppermute | solution.py:387
  57.7 0.7 copy-start.10
  57.7 1.0 copy-start.7
  58.7 34.1 %copy-start = (bf16[384,768]{1,0:T(8,128)(2,1)S(1)}, bf16[384,768]{1,0:T(8,128)(2,1)}, u32[]{:S(2)}) copy-start(bf16[384,768]{1,0:T(8,128)(2,1)} %up_ref.1) | copy-start | bytes 1769476
  58.7 34.1 %copy-start.1 = (bf16[8,24,1152]{2,1,0:T(8,128)(2,1)S(1)}, bf16[8,24,1152]{2,1,0:T(8,128)(2,1)}, u32[]{:S(2)}) copy-start(bf16[8,24,1152]{2,1,0:T(8,128)(2,1)} %get-tuple-element.37.set1) | copy-start | bytes 1327108
  58.7 34.1 %copy-start.2 = (bf16[8,24,1152]{2,1,0:T(8,128)(2,1)S(1)}, bf16[8,24,1152]{2,1,0:T(8,128)(2,1)}, u32[]{:S(2)}) copy-start(bf16[8,24,1152]{2,1,0:T(8,128)(2,1)} %get-tuple-element.38.set2) | copy-start | bytes 1327108
  76.8 16.0 %collective-permute-start.4 = (bf16[4,144,384]{2,1,0:T(8,128)(2,1)}, bf16[4,144,384]{2,1,0:T(8,128)(2,1)S(1)}, u32[]{:S(2)}, u32[]{:S(2)}) collective-permute-start(bf16[4,144,384]{2,1,0:T(8,128)(2,1)} %get-tuple-element.34), channel_id=1, source_target_pairs={{124,0},{0,4},{4,8},{8,12},{12,16},{16,20},{20,24},{24,28},{28,32}... | collective-permute-start | bytes 1327112 | tf_op jit(solution)/shard_map/ppermute | solution.py:387
  76.9 27.1 %all-to-all-start = ((bf16[128,18,128]{2,1,0:T(8,128)(2,1)}), bf16[128,18,128]{2,1,0:T(8,128)(2,1)S(1)}, u32[]{:S(2)}, u32[]{:S(2)}) async-start(bf16[128,18,128]{2,1,0:T(8,128)(2,1)} %get-tuple-element.33), calls=%async_computation | async-start | bytes 1572864 | tf_op jit(solution)/shard_map/all_to_all | solution.py:405
  92.8 1.0 copy-start.3
  93.8 1.0 copy-start.4

commit v3 on v2

--- a/solution.py
+++ b/solution.py
@@ -33,9 +33,28 @@
 
 
 def scaled_bias(bias_ref, table_ref, heads):
-    for h in range(heads):
-        for w in range(bias_ref.shape[1]):
-            table_ref[w * heads + h] = bias_ref[h, w].astype(F32) * LOG2E
+    count = bias_ref.shape[1]
+    stack = 8 // count
+    lane = lax.broadcasted_iota(jnp.int32, (8, 128), 1)
+
+    def eight(m, carry):
+        for g in range(heads // stack):
+            tiles = []
+            for i in range(9):
+                at = pl.multiple_of(m * 1152 + i * 128, 128)
+                parts = [bias_ref[g * stack + k, :, pl.ds(at, 128)].astype(F32) for k in range(stack)]
+                tiles.append(jnp.concatenate(parts, axis=0) * LOG2E)
+            for j in range(8):
+                main, tail = tiles[j], tiles[j + 1]
+                if j > 0:
+                    main = pltpu.roll(jnp.where(lane >= 16 * j, main, tail), 128 - 16 * j, axis=1)
+                    tail = pltpu.roll(tail, 128 - 16 * j, axis=1)
+                rows = pl.ds(g * 8 * 144 + m * 8 + j, 8, stride=144)
+                table_ref[0, rows, :] = main
+                table_ref[1, rows, :] = tail
+        return carry
+
+    lax.fori_loop(0, 18, eight, 0)
 
 
 def put_rows(ref, at, value):
@@ -84,7 +103,10 @@
             values = jnp.concatenate([v_all[rows, lanes], ones], axis=1)
             for j in range(min(4, heads - 4 * t)):
                 mine = (lane >= j * HD) & (lane < j * HD + HD)
-                s = mm(jnp.where(mine, q, jnp.zeros_like(q)), k, NT) + table_ref[w * heads + 4 * t + j]
+                first = ((4 * t + j) * (tokens // 144) + w) * 144
+                at = slice(first, first + 144)
+                bias = jnp.concatenate([table_ref[0, at, :], table_ref[1, at, :16]], axis=1)
+                s = mm(jnp.where(mine, q, jnp.zeros_like(q)), k, NT) + bias
                 p = jnp.exp2(s - jnp.max(s, axis=1, keepdims=True)).astype(BF)
                 o = mm(p, values)
                 total = jnp.where(mine, o[:, :128], total)
@@ -332,7 +354,7 @@
         scratch_shapes=[
             pltpu.VMEM((UNITS, 2, 576, 128), F32),
             pltpu.VMEM((UNITS, 2, 576, 128), F32),
-            pltpu.VMEM((24, 144, 144), F32),
+            pltpu.VMEM((2, 24 * 144, 128), F32),
             pltpu.VMEM((UNITS, 576, 256), BF),
             pltpu.VMEM((3, 192, 256), BF),
         ],
@@ -357,7 +379,7 @@
         scratch_shapes=[
             pltpu.VMEM((UNITS, 3, 288, 128), F32),
             pltpu.VMEM((UNITS, 3, 288, 128), F32),
-            pltpu.VMEM((24, 144, 144), F32),
+            pltpu.VMEM((2, 24 * 144, 128), F32),
             pltpu.VMEM((UNITS, 288, 384), BF),
             pltpu.VMEM((384, 768), F32),
         ],
@@ -419,11 +441,11 @@
     half = 6 * width
     halo = passed_along(field[:, :, :half], "lon", -1)
     fine_consts = (
-        fine_bias.reshape(fine_bias.shape[0], fine_bias.shape[1], 144, 144),
+        fine_bias,
         fine_gain_a, fine_qkv, fine_out, fine_gain_b, fine_in, fine_back, merge_gain, merge_weight,
     )
     coarse_consts = (
-        coarse_bias.reshape(coarse_bias.shape[0], coarse_bias.shape[1], 144, 144),
+        coarse_bias,
         coarse_gain_a, coarse_qkv, coarse_out, coarse_gain_b, coarse_in, coarse_back,
     )
     a_left, a_right, ca_left, ca_right = fine_call(field, 1, field, 2, fine_consts)

time: 126 us -> 125 us (level)
  local copies, waits for them, and re-layouts: 13.9 us -> 5.59 us
  Pallas kernels: 53 us -> 58.4 us
  waiting for transfers between devices: 15.7 us -> 18.2 us
    reshape x2 -> x0, local copies, waits for them, and re-layouts: 8.52 us -> none  [the longest x1 4.36 us: shards(): coarse_bias.reshape(coarse_bias.shape[0], coarse_bias.shape[1], 144, 144)]
    pallas_call x2, Pallas kernels: 30.8 us -> 34.2 us  [fine_call(): pl.pallas_call(fine_kernel, grid=(steps,), in_specs=[spec(left_at), spec(...]
    ppermute x5, waiting for transfers between devices: 9.29 us -> 11.8 us  [passed_along(): lax.ppermute(block, axis, [((i - distance) % n, i) for i in range(n)])]
    pallas_call x1, Pallas kernels: 18.1 us -> 20 us  [coarse_call(): pl.pallas_call(coarse_kernel, grid=(steps,), in_specs=[gspec] * 4 + [pl.B...]
    unnamed x22 -> x16, local copies, waits for them, and re-layouts: 3.04 us -> 3.32 us
  transfers between devices with their start and end apart: 6 -> 6, of which waited for: 3 -> 3; matrix products, arithmetic and copies ran while one was open for 8% -> 1% of each run, Pallas kernels for 41% -> 46%
where the time goes in v3:
time: 125 us
  Pallas kernels  58.4 us (47%)
  starting transfers between devices  21.9 us (18%)
  blocking collectives  20.3 us (16%)
  waiting for transfers between devices  18.2 us (15%)
  local copies, waits for them, and re-layouts  5.59 us (4%)
    pallas_call x2, Pallas kernels, fine_call(): pl.pallas_call(fine_kernel, grid=(steps,), in_specs=[spec(left_at), spec(...  34.2 us
    all_to_all x1, blocking collectives, reduce_everywhere(): lax.all_to_all(packed_call(sum_kernel, parts, packed.shape, BF), axes, 0, 0)  20.3 us
    pallas_call x1, Pallas kernels, coarse_call(): pl.pallas_call(coarse_kernel, grid=(steps,), in_specs=[gspec] * 4 + [pl.B...  20 us
    ppermute x5, waiting for transfers between devices, passed_along(): lax.ppermute(block, axis, [((i - distance) % n, i) for i in range(n)])  11.8 us
    ppermute x5, starting transfers between devices, passed_along(): lax.ppermute(block, axis, [((i - distance) % n, i) for i in range(n)])  11.4 us
    all_to_all x1, starting transfers between devices, reduce_everywhere(): parts = lax.all_to_all(packed, axes, 0, 0)  10.5 us
    all_to_all x1, waiting for transfers between devices, reduce_everywhere(): parts = lax.all_to_all(packed, axes, 0, 0)  6.36 us
    unnamed x16, local copies, waits for them, and re-layouts  3.32 us
  transfers between devices with their start and end apart: 6, of which 3 were waited for; matrix products, arithmetic and copies ran while one was open for 1% of the time, Pallas kernels for 46%

profile of v3, /device:TPU:1, one launch (start us, length us, event | category | flops | bytes accessed | tf_op | source)
XLA Modules:
  0.0 125.0 jit_solution(9891563649573941264)
XLA Ops:
  0.6 1.1 slice.6
  1.7 9.6 %collective-permute-start = (bf16[8,24,1152]{2,1,0:T(8,128)(2,1)S(1)}, bf16[8,24,1152]{2,1,0:T(8,128)(2,1)S(1)}, u32[]{:S(2)}, u32[]{:S(2)}) collective-permute-start(bf16[8,24,1152]{2,1,0:T(8,128)(2,1)S(1)} %slice.6), channel_id=1, source_target_pairs={{4,0},{8,4},{12,8},{16,12},{20,16},{24,20},{28,24},{32,28},{36,32}... | collective-permute-start | bytes 1327112 | tf_op jit(solution)/shard_map/ppermute | solution.py:409
  11.2 1.2 slice.7
  12.5 17.1 %shard_map.194 = (bf16[8,24,1152]{2,1,0:T(8,128)(2,1)}, bf16[8,24,1152]{2,1,0:T(8,128)(2,1)}, bf16[4,2,36,384]{3,2,1,0:T(8,128)(2,1)}, bf16[4,2,36,384]{3,2,1,0:T(8,128)(2,1)}) custom-call(bf16[8,24,4608]{2,1,0:T(8,128)(2,1)} %left_ref.3, bf16[8,24,4608]{2,1,0:T(8,128)(2,1)} %left_ref.3, bf16[6,4,20736]{2,1,0:T(4,128)(2,1)} %bias_ref.4, f32[192]{0:T(256)} %ga_ref.4, ...), custom_call_target="tpu_custom_call" | custom-call | flops 3000000000 | bytes 6000000 | tf_op jit(solution)/shard_map/pallas_call | solution.py:347
  29.6 0.0 collective-permute-done.right_ref
  29.6 0.0 copy-start.6
  29.6 0.2 collective-permute-start.2
  29.8 0.3 collective-permute-start.1
  30.1 0.3 copy-done.6
  30.4 17.1 %shard_map.195 = (bf16[8,24,1152]{2,1,0:T(8,128)(2,1)}, bf16[8,24,1152]{2,1,0:T(8,128)(2,1)}, bf16[4,2,36,384]{3,2,1,0:T(8,128)(2,1)}, bf16[4,2,36,384]{3,2,1,0:T(8,128)(2,1)}) custom-call(bf16[8,24,4608]{2,1,0:T(8,128)(2,1)} %left_ref.3, bf16[8,24,1152]{2,1,0:T(8,128)(2,1)} %copy-done.6, bf16[6,4,20736]{2,1,0:T(4,128)(2,1)} %bias_ref.4, f32[192]{0:T(256)} %ga_ref.4, ...), custom_call_target="tpu_custom_call" | custom-call | flops 3000000000 | bytes 6000000 | tf_op jit(solution)/shard_map/pallas_call | solution.py:347
  47.4 1.3 %collective-permute-start.3 = (bf16[8,24,1152]{2,1,0:T(8,128)(2,1)}, bf16[8,24,1152]{2,1,0:T(8,128)(2,1)S(1)}, u32[]{:S(2)}, u32[]{:S(2)}) collective-permute-start(bf16[8,24,1152]{2,1,0:T(8,128)(2,1)} %get-tuple-element.32), channel_id=1, source_target_pairs={{124,0},{0,4},{4,8},{8,12},{12,16},{16,20},{20,24},{24,28},{28,32}... | collective-permute-start | bytes 1327112 | tf_op jit(solution)/shard_map/ppermute | solution.py:409
  48.8 6.4 %collective-permute-done.1.g3 = bf16[4,2,36,384]{3,2,1,0:T(8,128)(2,1)S(1)} collective-permute-done((bf16[4,2,36,384]{3,2,1,0:T(8,128)(2,1)}, bf16[4,2,36,384]{3,2,1,0:T(8,128)(2,1)S(1)}, u32[]{:S(2)}, u32[]{:S(2)}) %collective-permute-start.1) | collective-permute-done | bytes 221216 | tf_op jit(solution)/shard_map/ppermute | solution.py:409
  55.1 0.0 copy-start.7
  55.1 0.0 collective-permute-done.2.cot_next_ref
  55.1 0.0 copy-start.5
  55.1 0.7 copy-done.7
  55.8 0.3 copy-done.5
  56.1 0.0 copy-start
  56.1 0.0 copy-start.1
  56.1 0.0 copy-start.2
  56.1 20.0 %shard_map.196 = (bf16[4,144,384]{2,1,0:T(8,128)(2,1)}, bf16[4,144,384]{2,1,0:T(8,128)(2,1)}, bf16[128,18,128]{2,1,0:T(8,128)(2,1)}) custom-call(bf16[4,2,36,384]{3,2,1,0:T(8,128)(2,1)} %get-tuple-element.22.g0, bf16[4,2,36,384]{3,2,1,0:T(8,128)(2,1)} %get-tuple-element.26.g1, bf16[4,2,36,384]{3,2,1,0:T(8,128)(2,1)} %get-tuple-element.27.g2, ...), custom_call_target="tpu_custom_call" | custom-call | flops 5000000000 | bytes 8000000 | tf_op jit(solution)/shard_map/pallas_call | solution.py:370
  76.2 0.1 collective-permute-start.4
  76.3 0.0 collective-permute-done.3.set0
  76.3 10.5 %all-to-all-start = ((bf16[128,18,128]{2,1,0:T(8,128)(2,1)}), bf16[128,18,128]{2,1,0:T(8,128)(2,1)S(1)}, u32[]{:S(2)}, u32[]{:S(2)}) async-start(bf16[128,18,128]{2,1,0:T(8,128)(2,1)} %get-tuple-element.33), calls=%async_computation | async-start | bytes 1572864 | tf_op jit(solution)/shard_map/all_to_all | solution.py:427
  86.7 5.4 %collective-permute-done.4.done_west = bf16[4,144,384]{2,1,0:T(8,128)(2,1)S(1)} collective-permute-done((bf16[4,144,384]{2,1,0:T(8,128)(2,1)}, bf16[4,144,384]{2,1,0:T(8,128)(2,1)S(1)}, u32[]{:S(2)}, u32[]{:S(2)}) %collective-permute-start.4) | collective-permute-done | bytes 442400 | tf_op jit(solution)/shard_map/ppermute | solution.py:409
  92.2 0.0 copy-done
  92.2 0.0 copy-done.1
  92.2 0.0 copy-done.2
  92.2 0.0 copy-start.3
  92.2 1.0 copy-done.3
  93.2 0.0 copy-start.4
  93.2 1.0 copy-done.4
  94.2 2.8 %shard_map.197 = bf16[8,24,4608]{2,1,0:T(8,128)(2,1)} custom-call(bf16[4,144,384]{2,1,0:T(8,128)(2,1)S(1)} %collective-permute-done.4.done_west, bf16[4,144,384]{2,1,0:T(8,128)(2,1)S(1)} %copy-done.4, bf16[8,24,1152]{2,1,0:T(8,128)(2,1)S(1)} %collective-permute-done.3.set0, bf16[8,24,1152]{2,1,0:T(8,128)(2,1)S(1)} %copy-done.1, ...), custom_call_target="tpu_custom_call" | custom-call | flops 99999997952 | bytes 6000000 | tf_op jit(solution)/shard_map/pallas_call | solution.py:395
  97.0 6.4 %all-to-all-done.in_ref = bf16[128,18,128]{2,1,0:T(8,128)(2,1)S(1)} async-done(((bf16[128,18,128]{2,1,0:T(8,128)(2,1)}), bf16[128,18,128]{2,1,0:T(8,128)(2,1)S(1)}, u32[]{:S(2)}, u32[]{:S(2)}) %all-to-all-start) | async-done | bytes 589856 | tf_op jit(solution)/shard_map/all_to_all | solution.py:427
  103.4 0.2 shard_map.198
  103.6 20.3 %all_to_all.10.in_ref = bf16[128,18,128]{2,1,0:T(8,128)(2,1)S(1)} all-to-all(bf16[128,18,128]{2,1,0:T(8,128)(2,1)S(1)} %shard_map.198), channel_id=1, replica_groups=mesh['lon'=32,'lat'=4] {'lon','lat'}, dimensions={0} | all-to-all | bytes 1179648 | tf_op jit(solution)/shard_map/all_to_all | solution.py:429
  123.9 1.1 shard_map.199
Async XLA Ops:
  1.7 27.9 %collective-permute-start = (bf16[8,24,1152]{2,1,0:T(8,128)(2,1)S(1)}, bf16[8,24,1152]{2,1,0:T(8,128)(2,1)S(1)}, u32[]{:S(2)}, u32[]{:S(2)}) collective-permute-start(bf16[8,24,1152]{2,1,0:T(8,128)(2,1)S(1)} %slice.6), channel_id=1, source_target_pairs={{4,0},{8,4},{12,8},{16,12},{20,16},{24,20},{28,24},{32,28},{36,32}... | collective-permute-start | bytes 1327112 | tf_op jit(solution)/shard_map/ppermute | solution.py:409
  29.6 0.8 copy-start.6
  29.6 25.5 %collective-permute-start.2 = (bf16[8,24,2304]{2,1,0:T(8,128)(2,1)S(1)}, bf16[8,24,2304]{2,1,0:T(8,128)(2,1)S(1)}, u32[]{:S(2)}, u32[]{:S(2)}) collective-permute-start(bf16[8,24,2304]{2,1,0:T(8,128)(2,1)S(1)} %slice.7), channel_id=1, source_target_pairs={{4,0},{8,4},{12,8},{16,12},{20,16},{24,20},{28,24},{32,28},{36,32}... | collective-permute-start | bytes 2654216 | tf_op jit(solution)/shard_map/ppermute | solution.py:409
  29.8 25.3 %collective-permute-start.1 = (bf16[4,2,36,384]{3,2,1,0:T(8,128)(2,1)}, bf16[4,2,36,384]{3,2,1,0:T(8,128)(2,1)S(1)}, u32[]{:S(2)}, u32[]{:S(2)}) collective-permute-start(bf16[4,2,36,384]{3,2,1,0:T(8,128)(2,1)} %get-tuple-element.28), channel_id=1, source_target_pairs={{4,0},{8,4},{12,8},{16,12},{20,16},{24,20},{28,24},{32,28},{36,32}... | collective-permute-start | bytes 663560 | tf_op jit(solution)/shard_map/ppermute | solution.py:409
  47.4 28.8 %collective-permute-start.3 = (bf16[8,24,1152]{2,1,0:T(8,128)(2,1)}, bf16[8,24,1152]{2,1,0:T(8,128)(2,1)S(1)}, u32[]{:S(2)}, u32[]{:S(2)}) collective-permute-start(bf16[8,24,1152]{2,1,0:T(8,128)(2,1)} %get-tuple-element.32), channel_id=1, source_target_pairs={{124,0},{0,4},{4,8},{8,12},{12,16},{16,20},{20,24},{24,28},{28,32}... | collective-permute-start | bytes 1327112 | tf_op jit(solution)/shard_map/ppermute | solution.py:409
  55.1 0.7 copy-start.7
  55.1 1.0 copy-start.5
  56.1 36.0 %copy-start = (bf16[384,768]{1,0:T(8,128)(2,1)S(1)}, bf16[384,768]{1,0:T(8,128)(2,1)}, u32[]{:S(2)}) copy-start(bf16[384,768]{1,0:T(8,128)(2,1)} %up_ref.1) | copy-start | bytes 1769476
  56.1 36.0 %copy-start.1 = (bf16[8,24,1152]{2,1,0:T(8,128)(2,1)S(1)}, bf16[8,24,1152]{2,1,0:T(8,128)(2,1)}, u32[]{:S(2)}) copy-start(bf16[8,24,1152]{2,1,0:T(8,128)(2,1)} %get-tuple-element.37.set1) | copy-start | bytes 1327108
  56.1 36.0 %copy-start.2 = (bf16[8,24,1152]{2,1,0:T(8,128)(2,1)S(1)}, bf16[8,24,1152]{2,1,0:T(8,128)(2,1)}, u32[]{:S(2)}) copy-start(bf16[8,24,1152]{2,1,0:T(8,128)(2,1)} %get-tuple-element.38.set2) | copy-start | bytes 1327108
  76.2 16.0 %collective-permute-start.4 = (bf16[4,144,384]{2,1,0:T(8,128)(2,1)}, bf16[4,144,384]{2,1,0:T(8,128)(2,1)S(1)}, u32[]{:S(2)}, u32[]{:S(2)}) collective-permute-start(bf16[4,144,384]{2,1,0:T(8,128)(2,1)} %get-tuple-element.34), channel_id=1, source_target_pairs={{124,0},{0,4},{4,8},{8,12},{12,16},{16,20},{20,24},{24,28},{28,32}... | collective-permute-start | bytes 1327112 | tf_op jit(solution)/shard_map/ppermute | solution.py:409
  76.3 27.1 %all-to-all-start = ((bf16[128,18,128]{2,1,0:T(8,128)(2,1)}), bf16[128,18,128]{2,1,0:T(8,128)(2,1)S(1)}, u32[]{:S(2)}, u32[]{:S(2)}) async-start(bf16[128,18,128]{2,1,0:T(8,128)(2,1)} %get-tuple-element.33), calls=%async_computation | async-start | bytes 1572864 | tf_op jit(solution)/shard_map/all_to_all | solution.py:427
  92.2 1.0 copy-start.3
  93.2 1.0 copy-start.4

commit v4 on v3

--- a/solution.py
+++ b/solution.py
@@ -229,7 +229,7 @@
 
 
 def coarse_kernel(
-    g0, g1, g2, g3, cot_ref, cot_next_ref, bias_ref, ga_ref, wqkv_ref, wo_ref, gb_ref,
+    g0, g1, g2, g3, cot_ref, cot_near_ref, cot_far_ref, bias_ref, ga_ref, wqkv_ref, wo_ref, gb_ref,
     wi_ref, wb_ref,
     done_own, done_next, packed_ref, nat_ref, win_ref, table_ref, mixed_ref, grad_ref,
 ):
@@ -244,7 +244,7 @@
     interleave(
         [
             coarse_unit(
-                u, (g0, g1, g2, g3), cot_ref, cot_next_ref, ga_ref, wqkv_ref, wo_ref, gb_ref, wi_ref, wb_ref,
+                u, (g0, g1, g2, g3), cot_ref, cot_near_ref, cot_far_ref, ga_ref, wqkv_ref, wo_ref, gb_ref, wi_ref, wb_ref,
                 done_own, done_next, grad_ref, nat_ref.at[u], win_ref.at[u], table_ref, mixed_ref.at[u],
             )
             for u in range(units)
@@ -277,7 +277,7 @@
 
 
 def coarse_unit(
-    u, groups, cot_ref, cot_next_ref, ga_ref, wqkv_ref, wo_ref, gb_ref, wi_ref, wb_ref,
+    u, groups, cot_ref, cot_near_ref, cot_far_ref, ga_ref, wqkv_ref, wo_ref, gb_ref, wi_ref, wb_ref,
     done_own, done_next, grad_ref, nat_ref, win_ref, table_ref, mixed_ref,
 ):
     width = wo_ref.shape[0]
@@ -301,12 +301,13 @@
         for t in range(3):
             nat_ref[t, pl.ds(src, 12, stride=12), :] = win_ref[t, dst : dst + 12, :]
     yield
-    for half, ref, out in ((0, cot_ref, done_own), (1, cot_next_ref, done_next)):
+    for half, out in enumerate((done_own, done_next)):
         tokens = jnp.concatenate([get_rows(nat_ref, l * 144 + half * 72, 72) for l in range(2)], axis=0).astype(BF)
         out[u] = tokens
         for l in range(2):
             for c in range(6):
-                put_rows(win_ref, (l * 6 + c) * 24, ref[2 * u + l, :, c * width : (c + 1) * width].astype(F32))
+                ref, at = (cot_ref, c) if half == 0 else (cot_near_ref, c) if c < 2 else (cot_far_ref, c - 2)
+                put_rows(win_ref, (l * 6 + c) * 24, ref[2 * u + l, :, at * width : (at + 1) * width].astype(F32))
         for r in range(2):
             x = get_every_other(win_ref, r, 144).astype(BF)
             grad_ref[:, r * width : (r + 1) * width] += mm(tokens, x, TN)
@@ -363,7 +364,7 @@
     )(left, right, *consts)
 
 
-def coarse_call(groups, cot, cot_next, consts):
+def coarse_call(groups, cot, cot_near, cot_far, consts):
     steps = groups[0].shape[0] // UNITS
     gspec = pl.BlockSpec((UNITS, 2, 36, 384), lambda i: (i, 0, 0, 0))
     dspec = pl.BlockSpec((UNITS, 144, 384), lambda i: (i, 0, 0))
@@ -371,7 +372,8 @@
         coarse_kernel,
         grid=(steps,),
         in_specs=[gspec] * 4
-        + [pl.BlockSpec((2 * UNITS, 24, 2304), lambda i: (i, 0, 1)), pl.BlockSpec((2 * UNITS, 24, 2304), lambda i: (i, 0, 0))]
+        + [pl.BlockSpec((2 * UNITS, 24, 2304), lambda i: (i, 0, 1)), pl.BlockSpec((2 * UNITS, 24, 768), lambda i: (i, 0, 0)),
+            pl.BlockSpec((2 * UNITS, 24, 1536), lambda i: (i, 0, 0))]
         + [whole(c) for c in consts],
         out_specs=[dspec, dspec, pl.BlockSpec((128, 18, 128), lambda i: (0, 0, 0))],
         out_shape=[jax.ShapeDtypeStruct((steps * UNITS, 144, 384), BF)] * 2
@@ -385,7 +387,7 @@
         ],
         compiler_params=params(56),
         cost_estimate=pl.CostEstimate(flops=5 * 10**9, bytes_accessed=8 * 10**6, transcendentals=10**6),
-    )(*groups, cot, cot_next, *consts)
+    )(*groups, cot, cot_near, cot_far, *consts)
 
 
 def final_call(done_west, done_east, quarters, up):
@@ -439,7 +441,9 @@
 ):
     width = fine_qkv.shape[0]
     half = 6 * width
+    near = 4 * width
     halo = passed_along(field[:, :, :half], "lon", -1)
+    cot_near = passed_along(cotangent[:, :, :near], "lon", -1)
     fine_consts = (
         fine_bias,
         fine_gain_a, fine_qkv, fine_out, fine_gain_b, fine_in, fine_back, merge_gain, merge_weight,
@@ -449,13 +453,13 @@
         coarse_gain_a, coarse_qkv, coarse_out, coarse_gain_b, coarse_in, coarse_back,
     )
     a_left, a_right, ca_left, ca_right = fine_call(field, 1, field, 2, fine_consts)
-    halo, ca_left, a_left = lax.optimization_barrier((halo, ca_left, a_left))
+    halo, cot_near, ca_left, a_left = lax.optimization_barrier((halo, cot_near, ca_left, a_left))
     ca_next = passed_along(ca_left, "lon", -1)
-    cot_first, a_left = lax.optimization_barrier((cotangent[:, :, : 2 * half], a_left))
-    cot_next = passed_along(cot_first, "lon", -1)
+    cot_rest, a_left = lax.optimization_barrier((cotangent[:, :, near : 2 * half], a_left))
+    cot_far = passed_along(cot_rest, "lon", -1)
     b_left, b_right, cb_left, cb_right = fine_call(field, 3, halo, 0, fine_consts)
     b_prev = passed_along(b_right, "lon", 1)
-    done_own, done_next, packed = coarse_call((ca_right, cb_left, cb_right, ca_next), cotangent, cot_next, coarse_consts)
+    done_own, done_next, packed = coarse_call((ca_right, cb_left, cb_right, ca_next), cotangent, cot_near, cot_far, coarse_consts)
     done_prev = passed_along(done_next, "lon", 1)
     packed, b_prev = lax.optimization_barrier((packed, b_prev))
     output = final_call(done_prev, done_own, (b_prev, a_left, a_right, b_left), up_weight)

time: 125 us -> 124 us (level)
  waiting for transfers between devices: 18.2 us -> 11.8 us
  starting transfers between devices: 21.9 us -> 26.3 us
    ppermute x5 -> x6, waiting for transfers between devices: 11.8 us -> 4.21 us  [passed_along(): lax.ppermute(block, axis, [((i - distance) % n, i) for i in range(n)])]
    ppermute x5 -> x6, starting transfers between devices: 11.4 us -> 15.3 us  [passed_along(): lax.ppermute(block, axis, [((i - distance) % n, i) for i in range(n)])]
    unnamed x16 -> x18, local copies, waits for them, and re-layouts: 3.32 us -> 2.92 us
  transfers between devices with their start and end apart: 6 -> 7, of which waited for: 3 -> 2; matrix products, arithmetic and copies ran while one was open for 1% -> 2% of each run, Pallas kernels for 46% -> 46%
where the time goes in v4:
time: 124 us
  Pallas kernels  58.4 us (47%)
  starting transfers between devices  26.3 us (21%)
  blocking collectives  20.3 us (16%)
  waiting for transfers between devices  11.8 us (10%)
  local copies, waits for them, and re-layouts  6.05 us (5%)
    pallas_call x2, Pallas kernels, fine_call(): pl.pallas_call(fine_kernel, grid=(steps,), in_specs=[spec(left_at), spec(...  34.2 us
    all_to_all x1, blocking collectives, reduce_everywhere(): lax.all_to_all(packed_call(sum_kernel, parts, packed.shape, BF), axes, 0, 0)  20.3 us
    pallas_call x1, Pallas kernels, coarse_call(): pl.pallas_call(coarse_kernel, grid=(steps,), in_specs=[gspec] * 4 + [pl.B...  20.1 us
    ppermute x6, starting transfers between devices, passed_along(): lax.ppermute(block, axis, [((i - distance) % n, i) for i in range(n)])  15.3 us
    all_to_all x1, starting transfers between devices, reduce_everywhere(): parts = lax.all_to_all(packed, axes, 0, 0)  11 us
    all_to_all x1, waiting for transfers between devices, reduce_everywhere(): parts = lax.all_to_all(packed, axes, 0, 0)  7.59 us
    ppermute x6, waiting for transfers between devices, passed_along(): lax.ppermute(block, axis, [((i - distance) % n, i) for i in range(n)])  4.21 us
    unnamed x18, local copies, waits for them, and re-layouts  2.92 us
  transfers between devices with their start and end apart: 7, of which 2 were waited for; matrix products, arithmetic and copies ran while one was open for 2% of the time, Pallas kernels for 46%

profile of v4, /device:TPU:1, one launch (start us, length us, event | category | flops | bytes accessed | tf_op | source)
XLA Modules:
  0.0 123.6 jit_solution(8574083916464657046)
XLA Ops:
  0.6 1.1 slice.9
  1.7 9.6 %collective-permute-start = (bf16[8,24,1152]{2,1,0:T(8,128)(2,1)S(1)}, bf16[8,24,1152]{2,1,0:T(8,128)(2,1)S(1)}, u32[]{:S(2)}, u32[]{:S(2)}) collective-permute-start(bf16[8,24,1152]{2,1,0:T(8,128)(2,1)S(1)} %slice.9), channel_id=1, source_target_pairs={{4,0},{8,4},{12,8},{16,12},{20,16},{24,20},{28,24},{32,28},{36,32}... | collective-permute-start | bytes 1327112 | tf_op jit(solution)/shard_map/ppermute | solution.py:411
  11.2 1.0 slice.10
  12.2 0.2 collective-permute-start.1
  12.4 1.1 slice.11
  13.5 17.1 %shard_map.194 = (bf16[8,24,1152]{2,1,0:T(8,128)(2,1)}, bf16[8,24,1152]{2,1,0:T(8,128)(2,1)}, bf16[4,2,36,384]{3,2,1,0:T(8,128)(2,1)}, bf16[4,2,36,384]{3,2,1,0:T(8,128)(2,1)}) custom-call(bf16[8,24,4608]{2,1,0:T(8,128)(2,1)} %left_ref.3, bf16[8,24,4608]{2,1,0:T(8,128)(2,1)} %left_ref.3, bf16[6,4,20736]{2,1,0:T(4,128)(2,1)} %bias_ref.4, f32[192]{0:T(256)} %ga_ref.4, ...), custom_call_target="tpu_custom_call" | custom-call | flops 3000000000 | bytes 6000000 | tf_op jit(solution)/shard_map/pallas_call | solution.py:348
  30.6 0.0 collective-permute-done.1.cot_near_ref
  30.7 0.0 copy-start.7
  30.7 0.0 collective-permute-done.right_ref
  30.7 0.0 copy-start.6
  30.7 3.7 %collective-permute-start.3 = (bf16[8,24,1536]{2,1,0:T(8,128)(2,1)S(1)}, bf16[8,24,1536]{2,1,0:T(8,128)(2,1)S(1)}, u32[]{:S(2)}, u32[]{:S(2)}) collective-permute-start(bf16[8,24,1536]{2,1,0:T(8,128)(2,1)S(1)} %slice.11), channel_id=1, source_target_pairs={{4,0},{8,4},{12,8},{16,12},{20,16},{24,20},{28,24},{32,28},{36,32}... | collective-permute-start | bytes 1769480 | tf_op jit(solution)/shard_map/ppermute | solution.py:411
  34.4 0.3 collective-permute-start.2
  34.7 0.0 copy-done.6
  34.7 17.1 %shard_map.195 = (bf16[8,24,1152]{2,1,0:T(8,128)(2,1)}, bf16[8,24,1152]{2,1,0:T(8,128)(2,1)}, bf16[4,2,36,384]{3,2,1,0:T(8,128)(2,1)}, bf16[4,2,36,384]{3,2,1,0:T(8,128)(2,1)}) custom-call(bf16[8,24,4608]{2,1,0:T(8,128)(2,1)} %left_ref.3, bf16[8,24,1152]{2,1,0:T(8,128)(2,1)} %copy-done.6, bf16[6,4,20736]{2,1,0:T(4,128)(2,1)} %bias_ref.4, f32[192]{0:T(256)} %ga_ref.4, ...), custom_call_target="tpu_custom_call" | custom-call | flops 3000000000 | bytes 6000000 | tf_op jit(solution)/shard_map/pallas_call | solution.py:348
  51.7 0.0 copy-done.7
  51.8 1.5 %collective-permute-start.4 = (bf16[8,24,1152]{2,1,0:T(8,128)(2,1)}, bf16[8,24,1152]{2,1,0:T(8,128)(2,1)S(1)}, u32[]{:S(2)}, u32[]{:S(2)}) collective-permute-start(bf16[8,24,1152]{2,1,0:T(8,128)(2,1)} %get-tuple-element.34), channel_id=1, source_target_pairs={{124,0},{0,4},{4,8},{8,12},{12,16},{16,20},{20,24},{24,28},{28,32}... | collective-permute-start | bytes 1327112 | tf_op jit(solution)/shard_map/ppermute | solution.py:411
  53.2 0.0 collective-permute-done.2.g3
  53.2 0.0 copy-start.8
  53.3 0.0 collective-permute-done.3.cot_far_ref
  53.3 0.0 copy-start.5
  53.3 0.7 copy-done.8
  53.9 0.2 copy-done.5
  54.1 0.0 copy-start
  54.1 0.0 copy-start.1
  54.2 0.0 copy-start.2
  54.2 20.1 %shard_map.196 = (bf16[4,144,384]{2,1,0:T(8,128)(2,1)}, bf16[4,144,384]{2,1,0:T(8,128)(2,1)}, bf16[128,18,128]{2,1,0:T(8,128)(2,1)}) custom-call(bf16[4,2,36,384]{3,2,1,0:T(8,128)(2,1)} %get-tuple-element.23.g0, bf16[4,2,36,384]{3,2,1,0:T(8,128)(2,1)} %get-tuple-element.27.g1, bf16[4,2,36,384]{3,2,1,0:T(8,128)(2,1)} %get-tuple-element.28.g2, ...), custom_call_target="tpu_custom_call" | custom-call | flops 5000000000 | bytes 8000000 | tf_op jit(solution)/shard_map/pallas_call | solution.py:371
  74.2 0.1 collective-permute-start.5
  74.3 0.0 collective-permute-done.4.set0
  74.3 11.0 %all-to-all-start = ((bf16[128,18,128]{2,1,0:T(8,128)(2,1)}), bf16[128,18,128]{2,1,0:T(8,128)(2,1)S(1)}, u32[]{:S(2)}, u32[]{:S(2)}) async-start(bf16[128,18,128]{2,1,0:T(8,128)(2,1)} %get-tuple-element.35), calls=%async_computation | async-start | bytes 1572864 | tf_op jit(solution)/shard_map/all_to_all | solution.py:429
  85.3 4.2 %collective-permute-done.5.done_west = bf16[4,144,384]{2,1,0:T(8,128)(2,1)S(1)} collective-permute-done((bf16[4,144,384]{2,1,0:T(8,128)(2,1)}, bf16[4,144,384]{2,1,0:T(8,128)(2,1)S(1)}, u32[]{:S(2)}, u32[]{:S(2)}) %collective-permute-start.5) | collective-permute-done | bytes 442400 | tf_op jit(solution)/shard_map/ppermute | solution.py:411
  89.5 0.0 copy-done
  89.5 0.0 copy-done.1
  89.5 0.0 copy-done.2
  89.5 0.0 copy-start.3
  89.5 1.0 copy-done.3
  90.5 0.0 copy-start.4
  90.5 1.0 copy-done.4
  91.6 2.8 %shard_map.197 = bf16[8,24,4608]{2,1,0:T(8,128)(2,1)} custom-call(bf16[4,144,384]{2,1,0:T(8,128)(2,1)S(1)} %collective-permute-done.5.done_west, bf16[4,144,384]{2,1,0:T(8,128)(2,1)S(1)} %copy-done.4, bf16[8,24,1152]{2,1,0:T(8,128)(2,1)S(1)} %collective-permute-done.4.set0, bf16[8,24,1152]{2,1,0:T(8,128)(2,1)S(1)} %copy-done.1, ...), custom_call_target="tpu_custom_call" | custom-call | flops 99999997952 | bytes 6000000 | tf_op jit(solution)/shard_map/pallas_call | solution.py:397
  94.4 7.6 %all-to-all-done.in_ref = bf16[128,18,128]{2,1,0:T(8,128)(2,1)S(1)} async-done(((bf16[128,18,128]{2,1,0:T(8,128)(2,1)}), bf16[128,18,128]{2,1,0:T(8,128)(2,1)S(1)}, u32[]{:S(2)}, u32[]{:S(2)}) %all-to-all-start) | async-done | bytes 589856 | tf_op jit(solution)/shard_map/all_to_all | solution.py:429
  102.0 0.2 shard_map.198
  102.2 20.3 %all_to_all.10.in_ref = bf16[128,18,128]{2,1,0:T(8,128)(2,1)S(1)} all-to-all(bf16[128,18,128]{2,1,0:T(8,128)(2,1)S(1)} %shard_map.198), channel_id=1, replica_groups=mesh['lon'=32,'lat'=4] {'lon','lat'}, dimensions={0} | all-to-all | bytes 1179648 | tf_op jit(solution)/shard_map/all_to_all | solution.py:431
  122.5 1.1 shard_map.199
Async XLA Ops:
  1.7 29.0 %collective-permute-start = (bf16[8,24,1152]{2,1,0:T(8,128)(2,1)S(1)}, bf16[8,24,1152]{2,1,0:T(8,128)(2,1)S(1)}, u32[]{:S(2)}, u32[]{:S(2)}) collective-permute-start(bf16[8,24,1152]{2,1,0:T(8,128)(2,1)S(1)} %slice.9), channel_id=1, source_target_pairs={{4,0},{8,4},{12,8},{16,12},{20,16},{24,20},{28,24},{32,28},{36,32}... | collective-permute-start | bytes 1327112 | tf_op jit(solution)/shard_map/ppermute | solution.py:411
  12.2 18.4 %collective-permute-start.1 = (bf16[8,24,768]{2,1,0:T(8,128)(2,1)S(1)}, bf16[8,24,768]{2,1,0:T(8,128)(2,1)S(1)}, u32[]{:S(2)}, u32[]{:S(2)}) collective-permute-start(bf16[8,24,768]{2,1,0:T(8,128)(2,1)S(1)} %slice.10), channel_id=1, source_target_pairs={{4,0},{8,4},{12,8},{16,12},{20,16},{24,20},{28,24},{32,28},{36,32}... | collective-permute-start | bytes 884744 | tf_op jit(solution)/shard_map/ppermute | solution.py:411
  30.7 21.1 %copy-start.7 = (bf16[8,24,768]{2,1,0:T(8,128)(2,1)}, bf16[8,24,768]{2,1,0:T(8,128)(2,1)S(1)}, u32[]{:S(2)}) copy-start(bf16[8,24,768]{2,1,0:T(8,128)(2,1)S(1)} %collective-permute-done.1.cot_near_ref) | copy-start | bytes 884740
  30.7 4.0 %copy-start.6 = (bf16[8,24,1152]{2,1,0:T(8,128)(2,1)}, bf16[8,24,1152]{2,1,0:T(8,128)(2,1)S(1)}, u32[]{:S(2)}) copy-start(bf16[8,24,1152]{2,1,0:T(8,128)(2,1)S(1)} %collective-permute-done.right_ref) | copy-start | bytes 1327108
  30.7 22.6 %collective-permute-start.3 = (bf16[8,24,1536]{2,1,0:T(8,128)(2,1)S(1)}, bf16[8,24,1536]{2,1,0:T(8,128)(2,1)S(1)}, u32[]{:S(2)}, u32[]{:S(2)}) collective-permute-start(bf16[8,24,1536]{2,1,0:T(8,128)(2,1)S(1)} %slice.11), channel_id=1, source_target_pairs={{4,0},{8,4},{12,8},{16,12},{20,16},{24,20},{28,24},{32,28},{36,32}... | collective-permute-start | bytes 1769480 | tf_op jit(solution)/shard_map/ppermute | solution.py:411
  34.4 18.9 %collective-permute-start.2 = (bf16[4,2,36,384]{3,2,1,0:T(8,128)(2,1)}, bf16[4,2,36,384]{3,2,1,0:T(8,128)(2,1)S(1)}, u32[]{:S(2)}, u32[]{:S(2)}) collective-permute-start(bf16[4,2,36,384]{3,2,1,0:T(8,128)(2,1)} %get-tuple-element.29), channel_id=1, source_target_pairs={{4,0},{8,4},{12,8},{16,12},{20,16},{24,20},{28,24},{32,28},{36,32}... | collective-permute-start | bytes 663560 | tf_op jit(solution)/shard_map/ppermute | solution.py:411
  51.8 22.6 %collective-permute-start.4 = (bf16[8,24,1152]{2,1,0:T(8,128)(2,1)}, bf16[8,24,1152]{2,1,0:T(8,128)(2,1)S(1)}, u32[]{:S(2)}, u32[]{:S(2)}) collective-permute-start(bf16[8,24,1152]{2,1,0:T(8,128)(2,1)} %get-tuple-element.34), channel_id=1, source_target_pairs={{124,0},{0,4},{4,8},{8,12},{12,16},{16,20},{20,24},{24,28},{28,32}... | collective-permute-start | bytes 1327112 | tf_op jit(solution)/shard_map/ppermute | solution.py:411
  53.2 0.7 copy-start.8
  53.3 0.9 copy-start.5
  54.1 35.4 %copy-start = (bf16[384,768]{1,0:T(8,128)(2,1)S(1)}, bf16[384,768]{1,0:T(8,128)(2,1)}, u32[]{:S(2)}) copy-start(bf16[384,768]{1,0:T(8,128)(2,1)} %up_ref.1) | copy-start | bytes 1769476
  54.1 35.4 %copy-start.1 = (bf16[8,24,1152]{2,1,0:T(8,128)(2,1)S(1)}, bf16[8,24,1152]{2,1,0:T(8,128)(2,1)}, u32[]{:S(2)}) copy-start(bf16[8,24,1152]{2,1,0:T(8,128)(2,1)} %get-tuple-element.39.set1) | copy-start | bytes 1327108
  54.2 35.4 %copy-start.2 = (bf16[8,24,1152]{2,1,0:T(8,128)(2,1)S(1)}, bf16[8,24,1152]{2,1,0:T(8,128)(2,1)}, u32[]{:S(2)}) copy-start(bf16[8,24,1152]{2,1,0:T(8,128)(2,1)} %get-tuple-element.40.set2) | copy-start | bytes 1327108
  74.2 15.3 %collective-permute-start.5 = (bf16[4,144,384]{2,1,0:T(8,128)(2,1)}, bf16[4,144,384]{2,1,0:T(8,128)(2,1)S(1)}, u32[]{:S(2)}, u32[]{:S(2)}) collective-permute-start(bf16[4,144,384]{2,1,0:T(8,128)(2,1)} %get-tuple-element.36), channel_id=1, source_target_pairs={{124,0},{0,4},{4,8},{8,12},{12,16},{16,20},{20,24},{24,28},{28,32}... | collective-permute-start | bytes 1327112 | tf_op jit(solution)/shard_map/ppermute | solution.py:411
  74.3 27.6 %all-to-all-start = ((bf16[128,18,128]{2,1,0:T(8,128)(2,1)}), bf16[128,18,128]{2,1,0:T(8,128)(2,1)S(1)}, u32[]{:S(2)}, u32[]{:S(2)}) async-start(bf16[128,18,128]{2,1,0:T(8,128)(2,1)} %get-tuple-element.35), calls=%async_computation | async-start | bytes 1572864 | tf_op jit(solution)/shard_map/all_to_all | solution.py:429
  89.5 1.0 copy-start.3
  90.5 1.0 copy-start.4

commit v5 on v4

--- a/solution.py
+++ b/solution.py
@@ -353,8 +353,8 @@
         out_shape=[jax.ShapeDtypeStruct((levels, rows, half), BF)] * 2
         + [jax.ShapeDtypeStruct((steps * UNITS, 2, 36, 384), BF)] * 2,
         scratch_shapes=[
-            pltpu.VMEM((UNITS, 2, 576, 128), F32),
-            pltpu.VMEM((UNITS, 2, 576, 128), F32),
+            pltpu.VMEM((UNITS, 2, 640, 128), F32),
+            pltpu.VMEM((UNITS, 2, 640, 128), F32),
             pltpu.VMEM((2, 24 * 144, 128), F32),
             pltpu.VMEM((UNITS, 576, 256), BF),
             pltpu.VMEM((3, 192, 256), BF),
@@ -379,8 +379,8 @@
         out_shape=[jax.ShapeDtypeStruct((steps * UNITS, 144, 384), BF)] * 2
         + [jax.ShapeDtypeStruct((128, 18, 128), BF)],
         scratch_shapes=[
-            pltpu.VMEM((UNITS, 3, 288, 128), F32),
-            pltpu.VMEM((UNITS, 3, 288, 128), F32),
+            pltpu.VMEM((UNITS, 3, 352, 128), F32),
+            pltpu.VMEM((UNITS, 3, 352, 128), F32),
             pltpu.VMEM((2, 24 * 144, 128), F32),
             pltpu.VMEM((UNITS, 288, 384), BF),
             pltpu.VMEM((384, 768), F32),

time: 124 us -> 124 us (level)
  no operation moved by 1% of the time
where the time goes in v5:
time: 124 us
  Pallas kernels  58.4 us (47%)
  starting transfers between devices  26.3 us (21%)
  blocking collectives  20.3 us (16%)
  waiting for transfers between devices  11.8 us (10%)
  local copies, waits for them, and re-layouts  6.05 us (5%)
    pallas_call x2, Pallas kernels, fine_call(): pl.pallas_call(fine_kernel, grid=(steps,), in_specs=[spec(left_at), spec(...  34.2 us
    all_to_all x1, blocking collectives, reduce_everywhere(): lax.all_to_all(packed_call(sum_kernel, parts, packed.shape, BF), axes, 0, 0)  20.3 us
    pallas_call x1, Pallas kernels, coarse_call(): pl.pallas_call(coarse_kernel, grid=(steps,), in_specs=[gspec] * 4 + [pl.B...  20.1 us
    ppermute x6, starting transfers between devices, passed_along(): lax.ppermute(block, axis, [((i - distance) % n, i) for i in range(n)])  15.3 us
    all_to_all x1, starting transfers between devices, reduce_everywhere(): parts = lax.all_to_all(packed, axes, 0, 0)  11 us
    all_to_all x1, waiting for transfers between devices, reduce_everywhere(): parts = lax.all_to_all(packed, axes, 0, 0)  7.59 us
    ppermute x6, waiting for transfers between devices, passed_along(): lax.ppermute(block, axis, [((i - distance) % n, i) for i in range(n)])  4.21 us
    unnamed x18, local copies, waits for them, and re-layouts  2.92 us
  transfers between devices with their start and end apart: 7, of which 2 were waited for; matrix products, arithmetic and copies ran while one was open for 2% of the time, Pallas kernels for 46%

profile of v5, /device:TPU:1, one launch (start us, length us, event | category | flops | bytes accessed | tf_op | source)
XLA Modules:
  0.0 123.6 jit_solution(12713730808084430693)
XLA Ops:
  0.6 1.1 slice.9
  1.7 9.6 %collective-permute-start = (bf16[8,24,1152]{2,1,0:T(8,128)(2,1)S(1)}, bf16[8,24,1152]{2,1,0:T(8,128)(2,1)S(1)}, u32[]{:S(2)}, u32[]{:S(2)}) collective-permute-start(bf16[8,24,1152]{2,1,0:T(8,128)(2,1)S(1)} %slice.9), channel_id=1, source_target_pairs={{4,0},{8,4},{12,8},{16,12},{20,16},{24,20},{28,24},{32,28},{36,32}... | collective-permute-start | bytes 1327112 | tf_op jit(solution)/shard_map/ppermute | solution.py:411
  11.2 1.0 slice.10
  12.2 0.2 collective-permute-start.1
  12.4 1.1 slice.11
  13.5 17.1 %shard_map.194 = (bf16[8,24,1152]{2,1,0:T(8,128)(2,1)}, bf16[8,24,1152]{2,1,0:T(8,128)(2,1)}, bf16[4,2,36,384]{3,2,1,0:T(8,128)(2,1)}, bf16[4,2,36,384]{3,2,1,0:T(8,128)(2,1)}) custom-call(bf16[8,24,4608]{2,1,0:T(8,128)(2,1)} %left_ref.3, bf16[8,24,4608]{2,1,0:T(8,128)(2,1)} %left_ref.3, bf16[6,4,20736]{2,1,0:T(4,128)(2,1)} %bias_ref.4, f32[192]{0:T(256)} %ga_ref.4, ...), custom_call_target="tpu_custom_call" | custom-call | flops 3000000000 | bytes 6000000 | tf_op jit(solution)/shard_map/pallas_call | solution.py:348
  30.6 0.0 collective-permute-done.1.cot_near_ref
  30.7 0.0 copy-start.7
  30.7 0.0 collective-permute-done.right_ref
  30.7 0.0 copy-start.6
  30.7 3.7 %collective-permute-start.3 = (bf16[8,24,1536]{2,1,0:T(8,128)(2,1)S(1)}, bf16[8,24,1536]{2,1,0:T(8,128)(2,1)S(1)}, u32[]{:S(2)}, u32[]{:S(2)}) collective-permute-start(bf16[8,24,1536]{2,1,0:T(8,128)(2,1)S(1)} %slice.11), channel_id=1, source_target_pairs={{4,0},{8,4},{12,8},{16,12},{20,16},{24,20},{28,24},{32,28},{36,32}... | collective-permute-start | bytes 1769480 | tf_op jit(solution)/shard_map/ppermute | solution.py:411
  34.4 0.3 collective-permute-start.2
  34.7 0.0 copy-done.6
  34.7 17.1 %shard_map.195 = (bf16[8,24,1152]{2,1,0:T(8,128)(2,1)}, bf16[8,24,1152]{2,1,0:T(8,128)(2,1)}, bf16[4,2,36,384]{3,2,1,0:T(8,128)(2,1)}, bf16[4,2,36,384]{3,2,1,0:T(8,128)(2,1)}) custom-call(bf16[8,24,4608]{2,1,0:T(8,128)(2,1)} %left_ref.3, bf16[8,24,1152]{2,1,0:T(8,128)(2,1)} %copy-done.6, bf16[6,4,20736]{2,1,0:T(4,128)(2,1)} %bias_ref.4, f32[192]{0:T(256)} %ga_ref.4, ...), custom_call_target="tpu_custom_call" | custom-call | flops 3000000000 | bytes 6000000 | tf_op jit(solution)/shard_map/pallas_call | solution.py:348
  51.7 0.0 copy-done.7
  51.8 1.5 %collective-permute-start.4 = (bf16[8,24,1152]{2,1,0:T(8,128)(2,1)}, bf16[8,24,1152]{2,1,0:T(8,128)(2,1)S(1)}, u32[]{:S(2)}, u32[]{:S(2)}) collective-permute-start(bf16[8,24,1152]{2,1,0:T(8,128)(2,1)} %get-tuple-element.34), channel_id=1, source_target_pairs={{124,0},{0,4},{4,8},{8,12},{12,16},{16,20},{20,24},{24,28},{28,32}... | collective-permute-start | bytes 1327112 | tf_op jit(solution)/shard_map/ppermute | solution.py:411
  53.2 0.0 collective-permute-done.2.g3
  53.2 0.0 copy-start.8
  53.3 0.0 collective-permute-done.3.cot_far_ref
  53.3 0.0 copy-start.5
  53.3 0.7 copy-done.8
  53.9 0.2 copy-done.5
  54.1 0.0 copy-start
  54.1 0.0 copy-start.1
  54.2 0.0 copy-start.2
  54.2 20.1 %shard_map.196 = (bf16[4,144,384]{2,1,0:T(8,128)(2,1)}, bf16[4,144,384]{2,1,0:T(8,128)(2,1)}, bf16[128,18,128]{2,1,0:T(8,128)(2,1)}) custom-call(bf16[4,2,36,384]{3,2,1,0:T(8,128)(2,1)} %get-tuple-element.23.g0, bf16[4,2,36,384]{3,2,1,0:T(8,128)(2,1)} %get-tuple-element.27.g1, bf16[4,2,36,384]{3,2,1,0:T(8,128)(2,1)} %get-tuple-element.28.g2, ...), custom_call_target="tpu_custom_call" | custom-call | flops 5000000000 | bytes 8000000 | tf_op jit(solution)/shard_map/pallas_call | solution.py:371
  74.2 0.1 collective-permute-start.5
  74.3 0.0 collective-permute-done.4.set0
  74.3 11.0 %all-to-all-start = ((bf16[128,18,128]{2,1,0:T(8,128)(2,1)}), bf16[128,18,128]{2,1,0:T(8,128)(2,1)S(1)}, u32[]{:S(2)}, u32[]{:S(2)}) async-start(bf16[128,18,128]{2,1,0:T(8,128)(2,1)} %get-tuple-element.35), calls=%async_computation | async-start | bytes 1572864 | tf_op jit(solution)/shard_map/all_to_all | solution.py:429
  85.3 4.2 %collective-permute-done.5.done_west = bf16[4,144,384]{2,1,0:T(8,128)(2,1)S(1)} collective-permute-done((bf16[4,144,384]{2,1,0:T(8,128)(2,1)}, bf16[4,144,384]{2,1,0:T(8,128)(2,1)S(1)}, u32[]{:S(2)}, u32[]{:S(2)}) %collective-permute-start.5) | collective-permute-done | bytes 442400 | tf_op jit(solution)/shard_map/ppermute | solution.py:411
  89.5 0.0 copy-done
  89.5 0.0 copy-done.1
  89.5 0.0 copy-done.2
  89.5 0.0 copy-start.3
  89.5 1.0 copy-done.3
  90.5 0.0 copy-start.4
  90.5 1.0 copy-done.4
  91.6 2.8 %shard_map.197 = bf16[8,24,4608]{2,1,0:T(8,128)(2,1)} custom-call(bf16[4,144,384]{2,1,0:T(8,128)(2,1)S(1)} %collective-permute-done.5.done_west, bf16[4,144,384]{2,1,0:T(8,128)(2,1)S(1)} %copy-done.4, bf16[8,24,1152]{2,1,0:T(8,128)(2,1)S(1)} %collective-permute-done.4.set0, bf16[8,24,1152]{2,1,0:T(8,128)(2,1)S(1)} %copy-done.1, ...), custom_call_target="tpu_custom_call" | custom-call | flops 99999997952 | bytes 6000000 | tf_op jit(solution)/shard_map/pallas_call | solution.py:397
  94.4 7.6 %all-to-all-done.in_ref = bf16[128,18,128]{2,1,0:T(8,128)(2,1)S(1)} async-done(((bf16[128,18,128]{2,1,0:T(8,128)(2,1)}), bf16[128,18,128]{2,1,0:T(8,128)(2,1)S(1)}, u32[]{:S(2)}, u32[]{:S(2)}) %all-to-all-start) | async-done | bytes 589856 | tf_op jit(solution)/shard_map/all_to_all | solution.py:429
  102.0 0.2 shard_map.198
  102.2 20.3 %all_to_all.10.in_ref = bf16[128,18,128]{2,1,0:T(8,128)(2,1)S(1)} all-to-all(bf16[128,18,128]{2,1,0:T(8,128)(2,1)S(1)} %shard_map.198), channel_id=1, replica_groups=mesh['lon'=32,'lat'=4] {'lon','lat'}, dimensions={0} | all-to-all | bytes 1179648 | tf_op jit(solution)/shard_map/all_to_all | solution.py:431
  122.5 1.1 shard_map.199
Async XLA Ops:
  1.7 29.0 %collective-permute-start = (bf16[8,24,1152]{2,1,0:T(8,128)(2,1)S(1)}, bf16[8,24,1152]{2,1,0:T(8,128)(2,1)S(1)}, u32[]{:S(2)}, u32[]{:S(2)}) collective-permute-start(bf16[8,24,1152]{2,1,0:T(8,128)(2,1)S(1)} %slice.9), channel_id=1, source_target_pairs={{4,0},{8,4},{12,8},{16,12},{20,16},{24,20},{28,24},{32,28},{36,32}... | collective-permute-start | bytes 1327112 | tf_op jit(solution)/shard_map/ppermute | solution.py:411
  12.2 18.4 %collective-permute-start.1 = (bf16[8,24,768]{2,1,0:T(8,128)(2,1)S(1)}, bf16[8,24,768]{2,1,0:T(8,128)(2,1)S(1)}, u32[]{:S(2)}, u32[]{:S(2)}) collective-permute-start(bf16[8,24,768]{2,1,0:T(8,128)(2,1)S(1)} %slice.10), channel_id=1, source_target_pairs={{4,0},{8,4},{12,8},{16,12},{20,16},{24,20},{28,24},{32,28},{36,32}... | collective-permute-start | bytes 884744 | tf_op jit(solution)/shard_map/ppermute | solution.py:411
  30.7 21.1 %copy-start.7 = (bf16[8,24,768]{2,1,0:T(8,128)(2,1)}, bf16[8,24,768]{2,1,0:T(8,128)(2,1)S(1)}, u32[]{:S(2)}) copy-start(bf16[8,24,768]{2,1,0:T(8,128)(2,1)S(1)} %collective-permute-done.1.cot_near_ref) | copy-start | bytes 884740
  30.7 4.0 %copy-start.6 = (bf16[8,24,1152]{2,1,0:T(8,128)(2,1)}, bf16[8,24,1152]{2,1,0:T(8,128)(2,1)S(1)}, u32[]{:S(2)}) copy-start(bf16[8,24,1152]{2,1,0:T(8,128)(2,1)S(1)} %collective-permute-done.right_ref) | copy-start | bytes 1327108
  30.7 22.6 %collective-permute-start.3 = (bf16[8,24,1536]{2,1,0:T(8,128)(2,1)S(1)}, bf16[8,24,1536]{2,1,0:T(8,128)(2,1)S(1)}, u32[]{:S(2)}, u32[]{:S(2)}) collective-permute-start(bf16[8,24,1536]{2,1,0:T(8,128)(2,1)S(1)} %slice.11), channel_id=1, source_target_pairs={{4,0},{8,4},{12,8},{16,12},{20,16},{24,20},{28,24},{32,28},{36,32}... | collective-permute-start | bytes 1769480 | tf_op jit(solution)/shard_map/ppermute | solution.py:411
  34.4 18.9 %collective-permute-start.2 = (bf16[4,2,36,384]{3,2,1,0:T(8,128)(2,1)}, bf16[4,2,36,384]{3,2,1,0:T(8,128)(2,1)S(1)}, u32[]{:S(2)}, u32[]{:S(2)}) collective-permute-start(bf16[4,2,36,384]{3,2,1,0:T(8,128)(2,1)} %get-tuple-element.29), channel_id=1, source_target_pairs={{4,0},{8,4},{12,8},{16,12},{20,16},{24,20},{28,24},{32,28},{36,32}... | collective-permute-start | bytes 663560 | tf_op jit(solution)/shard_map/ppermute | solution.py:411
  51.8 22.6 %collective-permute-start.4 = (bf16[8,24,1152]{2,1,0:T(8,128)(2,1)}, bf16[8,24,1152]{2,1,0:T(8,128)(2,1)S(1)}, u32[]{:S(2)}, u32[]{:S(2)}) collective-permute-start(bf16[8,24,1152]{2,1,0:T(8,128)(2,1)} %get-tuple-element.34), channel_id=1, source_target_pairs={{124,0},{0,4},{4,8},{8,12},{12,16},{16,20},{20,24},{24,28},{28,32}... | collective-permute-start | bytes 1327112 | tf_op jit(solution)/shard_map/ppermute | solution.py:411
  53.2 0.7 copy-start.8
  53.3 0.9 copy-start.5
  54.1 35.4 %copy-start = (bf16[384,768]{1,0:T(8,128)(2,1)S(1)}, bf16[384,768]{1,0:T(8,128)(2,1)}, u32[]{:S(2)}) copy-start(bf16[384,768]{1,0:T(8,128)(2,1)} %up_ref.1) | copy-start | bytes 1769476
  54.1 35.4 %copy-start.1 = (bf16[8,24,1152]{2,1,0:T(8,128)(2,1)S(1)}, bf16[8,24,1152]{2,1,0:T(8,128)(2,1)}, u32[]{:S(2)}) copy-start(bf16[8,24,1152]{2,1,0:T(8,128)(2,1)} %get-tuple-element.39.set1) | copy-start | bytes 1327108
  54.2 35.4 %copy-start.2 = (bf16[8,24,1152]{2,1,0:T(8,128)(2,1)S(1)}, bf16[8,24,1152]{2,1,0:T(8,128)(2,1)}, u32[]{:S(2)}) copy-start(bf16[8,24,1152]{2,1,0:T(8,128)(2,1)} %get-tuple-element.40.set2) | copy-start | bytes 1327108
  74.2 15.3 %collective-permute-start.5 = (bf16[4,144,384]{2,1,0:T(8,128)(2,1)}, bf16[4,144,384]{2,1,0:T(8,128)(2,1)S(1)}, u32[]{:S(2)}, u32[]{:S(2)}) collective-permute-start(bf16[4,144,384]{2,1,0:T(8,128)(2,1)} %get-tuple-element.36), channel_id=1, source_target_pairs={{124,0},{0,4},{4,8},{8,12},{12,16},{16,20},{20,24},{24,28},{28,32}... | collective-permute-start | bytes 1327112 | tf_op jit(solution)/shard_map/ppermute | solution.py:411
  74.3 27.6 %all-to-all-start = ((bf16[128,18,128]{2,1,0:T(8,128)(2,1)}), bf16[128,18,128]{2,1,0:T(8,128)(2,1)S(1)}, u32[]{:S(2)}, u32[]{:S(2)}) async-start(bf16[128,18,128]{2,1,0:T(8,128)(2,1)} %get-tuple-element.35), calls=%async_computation | async-start | bytes 1572864 | tf_op jit(solution)/shard_map/all_to_all | solution.py:429
  89.5 1.0 copy-start.3
  90.5 1.0 copy-start.4
